TPU v7x, 128 devices: a whole 4x4x4 slice. The times are simulated.
128 devices in a mesh: gx: 16 (over x, z), gy: 8 (over y, core).
Axes of the slice: x: 4, y: 4, z: 4, core: 2. Of those that a mesh axis runs over, the one named last changes fastest.
Arguments:
- positions: float32 [3, 2048, 256], P(None, ('gx', 'gy')), may hold values from 0 to 1
- velocities: float32 [3, 2048, 256], P(None, ('gx', 'gy')), may hold values from -6 to 6
- masses: float32 [2048, 256], P(('gx', 'gy')), may hold values from 0.004 to 0.016
- smoothing: float32 [2048, 256], P(('gx', 'gy')), may hold values from 0.35 to 0.6
- sound2: float32 [2048, 256], P(('gx', 'gy')), may hold values from 0.5 to 2
- counts: int32 [2048], P(('gx', 'gy')), may hold values from 64 to 256, as said below
- move_to: int32 [2048], P(('gx', 'gy')), may hold values from 0 to 2047, as said below
- proxy_send: int32 [16384], P(('gx', 'gy')), may hold values from 0 to 15
- pairs: int32 [20480, 3], P(('gx', 'gy')), may hold values from 0 to 143, as said below
Outputs:
- density: float32 [2048, 256], P(('gx', 'gy'))
- accel: float32 [3, 2048, 256], P(None, ('gx', 'gy'))
Inputs may be any that keep to these rules, and one draw needn't show every extreme that they name: `counts`: every cell holds at least 64 particles; some cell in every draw holds 256. move_to is a permutation; every cell stays on the same index of gy; one device hands at most 2 cells to any one device, and exactly 2 to each device it sends to. `pairs`: own cell numbers are below 16, source cells index the device's cell list (below 144), directions run from 0 to 26 with 13 the zero offset; each own cell has its zero-offset self pair and each proxy cell appears in exactly one pair.
All inputs are finite; a program needn't handle non-finite values.
Results may differ from a plain program's by a relative error of at most 0.0003.
Values sent between devices are 32-bit elements; how exact they have to be, the bound alone decides.
A program may use at most 64 MiB of HBM per device.

v0:
```python
import math

import jax
import jax.numpy as jnp
from jax import lax
from jax.sharding import PartitionSpec as P

CAP = 2


KERNEL_NORM = 21.0 / (16.0 * math.pi)
VISC_ALPHA = 1.0
VISC_BETA = 2.0
BLOCK_PAIRS = 8
HIGHEST = lax.Precision.HIGHEST


def from_behind(array, axis, by):
    size = lax.axis_size(axis)
    return lax.ppermute(array, axis, [(i, (i + by) % size) for i in range(size)])


def cell_offsets(direction):
    return jnp.stack([direction // 9 - 1, direction // 3 % 3 - 1, direction % 3 - 1]).astype(
        jnp.float32
    )


def one_hot(index, total):
    return (index[:, None] == jnp.arange(total, dtype=jnp.int32)[None, :]).astype(jnp.float32)


def select_cells(selector, fields):
    return jnp.einsum("bc,fcp->fbp", selector, fields, precision=HIGHEST)


def pair_geometry(block, here_pos, there_pos, here_smooth, there_smooth):
    shifted = there_pos + cell_offsets(block[:, 2])[:, :, None]
    separation = here_pos[:, :, :, None] - shifted[:, :, None, :]
    radius2 = jnp.sum(separation * separation, axis=0)
    length = 0.5 * (here_smooth[:, :, None] + there_smooth[:, None, :])
    ratio = jnp.sqrt(radius2) / length
    falloff = jnp.maximum(1.0 - 0.5 * ratio, 0.0)
    return (separation, radius2, length, ratio, falloff)


def density_sum(pair_list, cell_count, ifields, jfields):
    blocks = pair_list.reshape(-1, BLOCK_PAIRS, 3)
    source_total = jfields.shape[1]

    def density_step(total, block):
        target_hot = one_hot(block[:, 0], cell_count)
        picked_i = select_cells(target_hot, ifields)
        picked_j = select_cells(one_hot(block[:, 1], source_total), jfields)
        separation, radius2, length, ratio, falloff = pair_geometry(
            block, picked_i[0:3], picked_j[0:3], picked_i[3], picked_j[4]
        )
        kernel = KERNEL_NORM / length**3 * falloff**4 * (1.0 + 2.0 * ratio)
        contrib = jnp.sum(picked_j[3][:, None, :] * kernel, axis=2)
        return (total + jnp.einsum("bc,bp->cp", target_hot, contrib, precision=HIGHEST), None)

    start = jnp.zeros((cell_count, ifields.shape[2]), jnp.float32)
    return lax.scan(density_step, start, blocks)[0]


def force_sum(pair_list, cell_count, ifields, jfields):
    blocks = pair_list.reshape(-1, BLOCK_PAIRS, 3)
    source_total = jfields.shape[1]

    def force_step(total, block):
        target_hot = one_hot(block[:, 0], cell_count)
        picked_i = select_cells(target_hot, ifields)
        picked_j = select_cells(one_hot(block[:, 1], source_total), jfields)
        separation, radius2, length, ratio, falloff = pair_geometry(
            block, picked_i[0:3], picked_j[0:3], picked_i[6], picked_j[7]
        )
        gradient = -5.0 * KERNEL_NORM / length**5 * falloff**3
        relvel = picked_i[3:6][:, :, :, None] - picked_j[3:6][:, :, None, :]
        approach = jnp.minimum(jnp.sum(relvel * separation, axis=0), 0.0)
        compress = length * approach / (radius2 + 0.01 * length * length)
        sound_i = picked_i[7][:, :, None]
        sound_j = picked_j[8][None, :, :].reshape(picked_j.shape[1], 1, -1)
        rho_i = picked_i[8][:, :, None]
        rho_j = picked_j[9].reshape(picked_j.shape[1], 1, -1)
        speed = 0.5 * (jnp.sqrt(sound_i) + jnp.sqrt(sound_j))
        viscous = (-VISC_ALPHA * speed * compress + VISC_BETA * compress * compress) / (
            0.5 * (rho_i + rho_j)
        )
        factor = picked_j[6][:, None, :] * (sound_i / rho_i + sound_j / rho_j + viscous) * gradient
        contrib = -jnp.sum(factor[None] * separation, axis=3)
        return (total + jnp.einsum("bc,xbp->xcp", target_hot, contrib, precision=HIGHEST), None)

    start = jnp.zeros((3, cell_count, ifields.shape[2]), jnp.float32)
    return lax.scan(force_step, start, blocks)[0]


def earlier_same(group_key, order_key):
    same_group = group_key[:, None] == group_key[None, :]
    before = order_key[None, :] < order_key[:, None]
    return jnp.sum((same_group & before).astype(jnp.int32), axis=1)


def neighbour_halo(outgoing, along_columns, along_rows):
    field_count = outgoing.shape[0]
    slot_count = outgoing.shape[2]
    grouped = outgoing.reshape(field_count, 8, -1, slot_count)
    from_left = along_columns(grouped[:, 5:8], 1)
    from_right = along_columns(grouped[:, 0:3], -1)
    upward = along_rows(jnp.stack([grouped[:, 4], from_left[:, 2], from_right[:, 2]], 1), 1)
    downward = along_rows(jnp.stack([grouped[:, 3], from_left[:, 0], from_right[:, 0]], 1), -1)
    arranged = jnp.stack(
        [
            downward[:, 2],
            from_right[:, 1],
            upward[:, 2],
            downward[:, 0],
            upward[:, 0],
            downward[:, 1],
            from_left[:, 1],
            upward[:, 1],
        ],
        1,
    )
    return arranged.reshape(field_count, -1, slot_count)


def body(positions, velocities, masses, smoothing, sound2, counts, move_to, proxy_send, pairs):
    cell_count = masses.shape[0]
    slot_count = masses.shape[1]
    columns_gx = lax.axis_size("gx")
    columns_gy = lax.axis_size("gy")
    occupied = (
        lax.broadcasted_iota(jnp.int32, (cell_count, slot_count), 1) < counts[:, None]
    ).astype(jnp.float32)
    record = jnp.concatenate(
        [
            positions,
            velocities,
            (masses * occupied)[None],
            smoothing[None],
            sound2[None],
            occupied[None],
        ],
        0,
    )
    own_order = jnp.arange(cell_count, dtype=jnp.int32)
    dest_column = move_to // cell_count // columns_gy
    send_slot = dest_column * CAP + earlier_same(dest_column, own_order)
    buffer_count = columns_gx * CAP
    buffer_slots = jnp.arange(buffer_count, dtype=jnp.int32)
    matches = send_slot[None, :] == buffer_slots[:, None]
    filled_slot = jnp.any(matches, axis=1)
    outgoing = select_cells(matches.astype(jnp.float32), record)
    picked_number = jnp.sum(matches.astype(jnp.int32) * move_to[None, :], axis=1)
    new_numbers = jnp.where(filled_slot, picked_number, -1).astype(jnp.float32)
    arrived, arrived_numbers = (
        lax.all_to_all(outgoing, "gx", split_axis=1, concat_axis=1, tiled=True),
        lax.all_to_all(new_numbers[None, :, None], "gx", split_axis=1, concat_axis=1, tiled=True),
    )
    received = arrived_numbers[0, :, 0]
    new_local = jnp.where(received >= 0.0, received.astype(jnp.int32) % cell_count, -1)
    placed = (new_local[None, :] == own_order[:, None]).astype(jnp.float32)
    moved = select_cells(placed, arrived)
    filled = moved[9]
    proxy_hot = one_hot(proxy_send, cell_count)
    light_columns = lambda stacked, offset: from_behind(stacked, "gx", offset)
    light_rows = lambda stacked, offset: from_behind(stacked, "gy", offset)
    full_columns = lambda stacked, offset: from_behind(stacked, "gx", offset)
    full_rows = lambda stacked, offset: from_behind(stacked, "gy", offset)
    light = jnp.concatenate([moved[0:3], moved[6:8]], 0)
    remote = neighbour_halo(select_cells(proxy_hot, light), light_columns, light_rows)
    joined_light = jnp.concatenate([light, remote], 1)
    own_light = jnp.concatenate([moved[0:3], moved[7:8]], 0)
    jlight = jnp.concatenate([joined_light[0:3], joined_light[3:4], joined_light[4:5]], 0)
    rho = density_sum(pairs, cell_count, own_light, jlight)
    safe_rho = jnp.where(filled > 0, rho, 1.0)
    heavy = jnp.concatenate([moved[0:9], safe_rho[None]], 0)
    remote_all = neighbour_halo(select_cells(proxy_hot, heavy), full_columns, full_rows)
    joined = jnp.concatenate([heavy, remote_all], 1)
    own_fields = jnp.concatenate([moved[0:6], moved[7:9], safe_rho[None]], 0)
    accel = force_sum(pairs, cell_count, own_fields, joined)
    return (rho * filled, accel * filled[None])


def solution(mesh):
    placed = (
        P(None, ("gx", "gy"), None),
        P(None, ("gx", "gy"), None),
        P(("gx", "gy"), None),
        P(("gx", "gy"), None),
        P(("gx", "gy"), None),
        P(("gx", "gy")),
        P(("gx", "gy")),
        P(("gx", "gy")),
        P(("gx", "gy"), None),
    )
    return jax.shard_map(
        body,
        mesh=mesh,
        in_specs=placed,
        out_specs=(P(("gx", "gy"), None), P(None, ("gx", "gy"), None)),
        check_vma=False,
    )
```

profile of v0, /device:TPU:0, one launch (start us, length us, event | category | flops | bytes accessed | tf_op | source)
XLA Modules:
  0.0 361.9 jit_solution(1464019013054460076)
XLA Ops:
  3.7 8.0 %all-to-all-start.1 = ((f32[1,32,1]{2,0,1:T(1,128)}), f32[1,32,1]{2,0,1:T(1,128)S(1)}, u32[]{:S(2)}, u32[]{:S(2)}) async-start(f32[1,32,1]{2,0,1:T(1,128)} %copy.24), calls=%async_computation.1 | async-start | bytes 32768 | tf_op jit(solution)/shard_map/all_to_all | solution.py:158
  19.3 5.6 %all-to-all-start = ((f32[10,32,256]{2,0,1:T(8,128)}), f32[10,32,256]{2,0,1:T(8,128)S(1)}, u32[]{:S(2)}, u32[]{:S(2)}) async-start(f32[10,32,256]{2,0,1:T(8,128)} %copy.23), calls=%async_computation | async-start | bytes 1048576 | tf_op jit(solution)/shard_map/all_to_all | solution.py:157
  26.2 9.6 %all-to-all-done = f32[10,32,256]{2,0,1:T(8,128)S(1)} async-done(((f32[10,32,256]{2,0,1:T(8,128)}), f32[10,32,256]{2,0,1:T(8,128)S(1)}, u32[]{:S(2)}, u32[]{:S(2)}) %all-to-all-start) | async-done | bytes 327712 | tf_op jit(solution)/shard_map/all_to_all | solution.py:157
  37.4 4.8 %collective-permute-start.1 = (f32[5,3,16,256]{3,2,1,0:T(8,128)S(1)}, f32[5,3,16,256]{3,2,1,0:T(8,128)S(1)}, u32[]{:S(2)}, u32[]{:S(2)}) collective-permute-start(f32[5,3,16,256]{3,2,1,0:T(8,128)S(1)} %get-tuple-element.340), channel_id=1, source_target_pairs={{0,120},{8,0},{16,8},{24,16},{32,24},{40,32},{48,40},{56,48},{64,5... | collective-permute-start | bytes 737288 | tf_op jit(solution)/shard_map/ppermute | solution.py:20
  42.2 4.2 %collective-permute-done = f32[5,3,16,256]{3,2,1,0:T(8,128)S(1)} collective-permute-done((f32[5,3,16,256]{3,2,1,0:T(8,128)S(1)}, f32[5,3,16,256]{3,2,1,0:T(8,128)S(1)}, u32[]{:S(2)}, u32[]{:S(2)}) %collective-permute-start) | collective-permute-done | bytes 245792 | tf_op jit(solution)/shard_map/ppermute | solution.py:20
  52.1 5.1 %collective-permute-done.3 = f32[5,3,16,256]{3,2,1,0:T(8,128)S(1)} collective-permute-done((f32[5,3,16,256]{3,2,1,0:T(8,128)S(1)}, f32[5,3,16,256]{3,2,1,0:T(8,128)S(1)}, u32[]{:S(2)}, u32[]{:S(2)}) %collective-permute-start.3) | collective-permute-done | bytes 245792 | tf_op jit(solution)/shard_map/ppermute | solution.py:20
  57.4 89.2 %while.28 = (s32[]{:T(128)}, f32[16,256]{1,0:T(8,128)S(1)}, s32[20,8,3]{1,2,0:T(4,128)S(1)}, f32[5,144,256]{2,1,0:T(8,128)S(1)}, f32[4,16,256]{2,1,0:T(8,128)S(1)}, /*index=5*/s32[]{:T(128)}, s32[]{:T(128)}) while((s32[]{:T(128)}, f32[16,256]{1,0:T(8,128)S(1)}, s32[20,8,3]{1,2,0:T(4,128)S(1)}, f32[5,144,256]{2,1,0:T(8,128)S(1)}, ...), condition=%wide.region_6.7_spmd.clone, body=%wide.region_3.6_spmd.clone.sunk | while | flops 32781984 | bytes 5342107 | solution.py:63
  148.1 5.4 %collective-permute-start.5 = (f32[10,3,16,256]{3,2,1,0:T(8,128)S(1)}, f32[10,3,16,256]{3,2,1,0:T(8,128)S(1)}, u32[]{:S(2)}, u32[]{:S(2)}) collective-permute-start(f32[10,3,16,256]{3,2,1,0:T(8,128)S(1)} %get-tuple-element.336), channel_id=1, source_target_pairs={{0,120},{8,0},{16,8},{24,16},{32,24},{40,32},{48,40},{56,48},{64,5... | collective-permute-start | bytes 1474568 | tf_op jit(solution)/shard_map/ppermute | solution.py:20
  153.4 9.3 %collective-permute-done.4 = f32[10,3,16,256]{3,2,1,0:T(8,128)S(1)} collective-permute-done((f32[10,3,16,256]{3,2,1,0:T(8,128)S(1)}, f32[10,3,16,256]{3,2,1,0:T(8,128)S(1)}, u32[]{:S(2)}, u32[]{:S(2)}) %collective-permute-start.4) | collective-permute-done | bytes 491552 | tf_op jit(solution)/shard_map/ppermute | solution.py:20
  162.9 6.3 %collective-permute-done.6 = f32[10,3,16,256]{3,2,1,0:T(8,128)S(1)} collective-permute-done((f32[10,3,16,256]{3,2,1,0:T(8,128)S(1)}, f32[10,3,16,256]{3,2,1,0:T(8,128)S(1)}, u32[]{:S(2)}, u32[]{:S(2)}) %collective-permute-start.6) | collective-permute-done | bytes 491552 | tf_op jit(solution)/shard_map/ppermute | solution.py:20
  171.9 8.0 %collective-permute-done.7 = f32[10,3,16,256]{3,2,1,0:T(8,128)S(1)} collective-permute-done((f32[10,3,16,256]{3,2,1,0:T(8,128)}, f32[10,3,16,256]{3,2,1,0:T(8,128)S(1)}, u32[]{:S(2)}, u32[]{:S(2)}) %collective-permute-start.7) | collective-permute-done | bytes 491552 | tf_op jit(solution)/shard_map/ppermute | solution.py:20
  180.2 181.1 %while.29 = (s32[]{:T(128)}, f32[3,16,256]{2,1,0:T(8,128)S(1)}, s32[20,8,3]{1,2,0:T(4,128)S(1)}, f32[10,144,256]{2,1,0:T(8,128)S(1)}, f32[9,16,256]{2,1,0:T(8,128)S(1)}, /*index=5*/s32[]{:T(128)}, s32[]{:T(128)}) while((s32[]{:T(128)}, f32[3,16,256]{2,1,0:T(8,128)S(1)}, s32[20,8,3]{1,2,0:T(4,128)S(1)}, ...), condition=%wide.region_11.12_spmd.clone, body=%wide.region_7.11_spmd.clone.sunk | while | flops 69504672 | bytes 15074203 | solution.py:94
  183.5 3.6 fusion.136
  192.5 3.6 fusion.136
  201.6 3.6 fusion.136
  210.6 3.6 fusion.136
  219.7 3.6 fusion.136
  228.7 3.6 fusion.136
  237.8 3.6 fusion.136
  246.8 3.6 fusion.136
  255.9 3.6 fusion.136
  264.9 3.6 fusion.136
  274.0 3.6 fusion.136
  283.0 3.6 fusion.136
  292.1 3.6 fusion.136
  301.1 3.6 fusion.136
  310.2 3.6 fusion.136
  319.2 3.6 fusion.136
  328.3 3.6 fusion.136
  337.4 3.6 fusion.136
  346.4 3.6 fusion.136
  355.5 3.6 fusion.136
  (558 shorter events, 220.4 us)
Async XLA Ops:
  0.6 35.6 %copy-start.1 = (s32[128]{0:T(128)S(1)}, s32[128]{0:T(128)}, u32[]{:S(2)}) copy-start(s32[128]{0:T(128)} %param.20) | copy-start | bytes 1540
  3.7 15.6 %all-to-all-start.1 = ((f32[1,32,1]{2,0,1:T(1,128)}), f32[1,32,1]{2,0,1:T(1,128)S(1)}, u32[]{:S(2)}, u32[]{:S(2)}) async-start(f32[1,32,1]{2,0,1:T(1,128)} %copy.24), calls=%async_computation.1 | async-start | bytes 32768 | tf_op jit(solution)/shard_map/all_to_all | solution.py:158
  19.3 16.5 %all-to-all-start = ((f32[10,32,256]{2,0,1:T(8,128)}), f32[10,32,256]{2,0,1:T(8,128)S(1)}, u32[]{:S(2)}, u32[]{:S(2)}) async-start(f32[10,32,256]{2,0,1:T(8,128)} %copy.23), calls=%async_computation | async-start | bytes 1048576 | tf_op jit(solution)/shard_map/all_to_all | solution.py:157
  24.9 21.6 %copy-start = (s32[160,3]{0,1:T(4,128)S(1)}, s32[160,3]{0,1:T(4,128)}, u32[]{:S(2)}) copy-start(s32[160,3]{0,1:T(4,128)} %param.21) | copy-start | bytes 5764
  36.8 9.6 %collective-permute-start = (f32[5,3,16,256]{3,2,1,0:T(8,128)S(1)}, f32[5,3,16,256]{3,2,1,0:T(8,128)S(1)}, u32[]{:S(2)}, u32[]{:S(2)}) collective-permute-start(f32[5,3,16,256]{3,2,1,0:T(8,128)S(1)} %get-tuple-element.339), channel_id=1, source_target_pairs={{0,8},{8,16},{16,24},{24,32},{32,40},{40,48},{48,56},{56,64},{64,7... | collective-permute-start | bytes 737288 | tf_op jit(solution)/shard_map/ppermute | solution.py:20
  37.4 9.0 %collective-permute-start.1 = (f32[5,3,16,256]{3,2,1,0:T(8,128)S(1)}, f32[5,3,16,256]{3,2,1,0:T(8,128)S(1)}, u32[]{:S(2)}, u32[]{:S(2)}) collective-permute-start(f32[5,3,16,256]{3,2,1,0:T(8,128)S(1)} %get-tuple-element.340), channel_id=1, source_target_pairs={{0,120},{8,0},{16,8},{24,16},{32,24},{40,32},{48,40},{56,48},{64,5... | collective-permute-start | bytes 737288 | tf_op jit(solution)/shard_map/ppermute | solution.py:20
  46.4 3.7 %collective-permute-start.2 = (f32[5,3,16,256]{3,2,1,0:T(8,128)S(1)}, f32[5,3,16,256]{3,2,1,0:T(8,128)S(1)}, u32[]{:S(2)}, u32[]{:S(2)}) collective-permute-start(f32[5,3,16,256]{3,2,1,0:T(8,128)S(1)} %pad_maximum_fusion.4), channel_id=1, source_target_pairs={{0,7},{1,0},{2,1},{3,2},{4,3},{5,4},{6,5},{7,6},{8,15},{9,8},{10,9... | collective-permute-start | bytes 737288 | tf_op jit(solution)/shard_map/ppermute | solution.py:20
  50.2 7.0 %collective-permute-start.3 = (f32[5,3,16,256]{3,2,1,0:T(8,128)S(1)}, f32[5,3,16,256]{3,2,1,0:T(8,128)S(1)}, u32[]{:S(2)}, u32[]{:S(2)}) collective-permute-start(f32[5,3,16,256]{3,2,1,0:T(8,128)S(1)} %pad_maximum_fusion.5), channel_id=1, source_target_pairs={{0,1},{1,2},{2,3},{3,4},{4,5},{5,6},{6,7},{7,0},{8,9},{9,10},{10,1... | collective-permute-start | bytes 737288 | tf_op jit(solution)/shard_map/ppermute | solution.py:20
  148.0 14.8 %collective-permute-start.4 = (f32[10,3,16,256]{3,2,1,0:T(8,128)S(1)}, f32[10,3,16,256]{3,2,1,0:T(8,128)S(1)}, u32[]{:S(2)}, u32[]{:S(2)}) collective-permute-start(f32[10,3,16,256]{3,2,1,0:T(8,128)S(1)} %get-tuple-element.335), channel_id=1, source_target_pairs={{0,8},{8,16},{16,24},{24,32},{32,40},{40,48},{48,56},{56,64},{64,7... | collective-permute-start | bytes 1474568 | tf_op jit(solution)/shard_map/ppermute | solution.py:20
  148.1 14.7 %collective-permute-start.5 = (f32[10,3,16,256]{3,2,1,0:T(8,128)S(1)}, f32[10,3,16,256]{3,2,1,0:T(8,128)S(1)}, u32[]{:S(2)}, u32[]{:S(2)}) collective-permute-start(f32[10,3,16,256]{3,2,1,0:T(8,128)S(1)} %get-tuple-element.336), channel_id=1, source_target_pairs={{0,120},{8,0},{16,8},{24,16},{32,24},{40,32},{48,40},{56,48},{64,5... | collective-permute-start | bytes 1474568 | tf_op jit(solution)/shard_map/ppermute | solution.py:20
  162.8 6.4 %collective-permute-start.6 = (f32[10,3,16,256]{3,2,1,0:T(8,128)S(1)}, f32[10,3,16,256]{3,2,1,0:T(8,128)S(1)}, u32[]{:S(2)}, u32[]{:S(2)}) collective-permute-start(f32[10,3,16,256]{3,2,1,0:T(8,128)S(1)} %pad_maximum_fusion.2), channel_id=1, source_target_pairs={{0,7},{1,0},{2,1},{3,2},{4,3},{5,4},{6,5},{7,6},{8,15},{9,8},{10,9... | collective-permute-start | bytes 1474568 | tf_op jit(solution)/shard_map/ppermute | solution.py:20
  170.1 9.8 %collective-permute-start.7 = (f32[10,3,16,256]{3,2,1,0:T(8,128)}, f32[10,3,16,256]{3,2,1,0:T(8,128)S(1)}, u32[]{:S(2)}, u32[]{:S(2)}) collective-permute-start(f32[10,3,16,256]{3,2,1,0:T(8,128)} %pad_maximum_fusion.3), channel_id=1, source_target_pairs={{0,1},{1,2},{2,3},{3,4},{4,5},{5,6},{6,7},{7,0},{8,9},{9,10},{10,1... | collective-permute-start | bytes 1474568 | tf_op jit(solution)/shard_map/ppermute | solution.py:20
where the time goes:
time: 362 us
  other arithmetic  235 us (65%)
  waiting for transfers between devices  47.6 us (13%)
  matrix products  40.5 us (11%)
  starting transfers between devices  28.2 us (8%)
  local copies, waits for them, and re-layouts  6.12 us (2%)
    mul x20, other arithmetic, force_step(): picked_j[6][:, None, :] * (sound_i / rho_i + sound_j / rho_j + viscous)  71.2 us
    reduce_sum x20, other arithmetic, density_step(): contrib = jnp.sum(picked_j[3][:, None, :] * kernel, axis=2)  46.4 us
    reduce_sum x20, other arithmetic, force_step(): approach = jnp.minimum(jnp.sum(relvel * separation, axis=0), 0.0)  45.1 us
    reduce_sum x20, other arithmetic, force_step(): contrib = -jnp.sum(factor[None] * separation, axis=3)  37.8 us
    ppermute x8, waiting for transfers between devices, from_behind(): lax.ppermute(array, axis, [(i, (i + by) % size) for i in range(size)])  36.4 us
    dot_general x84, matrix products, select_cells(): return jnp.einsum('bc,fcp->fbp', selector, fields, precision=HIGHEST)  29.8 us
    reduce_sum x20, other arithmetic, pair_geometry(): radius2 = jnp.sum(separation * separation, axis=0)  22.4 us
    ppermute x8, starting transfers between devices, from_behind(): lax.ppermute(array, axis, [(i, (i + by) % size) for i in range(size)])  14.6 us
  transfers between devices with their start and end apart: 10, of which 8 were waited for; matrix products, arithmetic and copies ran while one was open for 2% of the time, Pallas kernels for 0%

commit v1 on v0

v1 whole, which is shorter than its diff:
```python
import math, functools
import jax, jax.numpy as jnp
from jax import lax
from jax.experimental import pallas as pl
from jax.experimental.pallas import tpu as pltpu

CELLS=16; SLOTS=256; NPAIRS=160; NORM=21.0/(16.0*math.pi)
MAXT=2*NPAIRS+CELLS+8
FIRST=2*NPAIRS

def rcp(x, approx=True):
    return pl.reciprocal(x, approx=approx)

def append(buf, x0, x1, pos, lane):
    tile=lax.shift_right_logical(pos,7); s=lax.bitwise_and(pos,127)
    t0=pltpu.roll(x0,s,1); t1=pltpu.roll(x1,s,1)
    keep=lane>=s
    buf[tile]=jnp.where(keep,t0,buf[tile])
    buf[tile+1]=jnp.where(keep,t1,t0)
    buf[tile+2]=jnp.where(keep,0.0,t1)

def plan(meta, pairs, tab, head, link):
    for a in range(CELLS):
        head[a]=-1
    def chain(p,_):
        a=pairs[3*p]
        link[p]=head[a]
        head[a]=p
        return 0
    lax.fori_loop(0,NPAIRS,chain,0)

def pack_main(rec, meta, pairs, tab, head, link, buf):
    lane=lax.broadcasted_iota(jnp.int32,(8,128),1)
    row=lax.broadcasted_iota(jnp.int32,(8,128),0)
    def cell(a,carry):
        k,tile=carry
        tab[FIRST+a]=tile
        def cond(c): return c[0]>=0
        def step(c):
            p,k,pos=c
            b=pairs[3*p+1]; d=pairs[3*p+2]
            n=lax.shift_right_logical(b,4)
            r=lax.bitwise_and(b,15)
            cell_=jnp.where(n==0,r,meta[n*128+16+r])
            src=n*16+cell_
            count=meta[n*128+cell_]
            tab[k]=src; tab[NPAIRS+k]=pos
            dx=d//9; dy=d//3-3*dx; dz=d-3*(d//3)
            shift=jnp.where(row==0,dx,jnp.where(row==1,dy,dz))-1
            shift=jnp.where(row<3,shift,0).astype(jnp.float32)
            append(buf,rec[src,:,0:128]+shift,rec[src,:,128:256]+shift,pos,lane)
            return link[p],k+1,pos+count
        _,k,pos=lax.while_loop(cond,step,(head[a],k,tile*128))
        return k,lax.shift_right_logical(pos+127,7)
    _,tile=lax.fori_loop(0,CELLS,cell,(0,0))
    tab[FIRST+CELLS]=tile

def spread(dst, f, rows):
    dst[f]=jnp.broadcast_to(rows.T,(SLOTS,128))

def density_kernel(IB,JB,approx,rec,meta,pairs,rho,safe,tab,buf,head,link,icol,acc):
    plan(meta,pairs,tab,head,link)
    pack_main(rec,meta,pairs,tab,head,link,buf)
    def cell(a,_):
        cols=rec[a].T
        for f,rw in enumerate((0,1,2,4)):
            icol[f]=jnp.broadcast_to(cols[:,rw:rw+1],(SLOTS,128))
        first=tab[FIRST+a]; last=tab[FIRST+a+1]
        nfull=(last-first)//JB
        count=meta[a]
        def iblock(g,_):
            rows=pl.ds(pl.multiple_of(g*IB,IB),IB)
            xi,yi,zi,hi=(icol[f,rows,:] for f in range(4))
            def tile(t):
                j=lambda rw: buf[t,rw:rw+1,:]
                dx=xi-j(0); dy=yi-j(1); dz=zi-j(2)
                r2=dx*dx+dy*dy+dz*dz
                s=hi+j(4)
                inv=rcp(s,approx)
                r=r2*lax.rsqrt(jnp.maximum(r2,1e-30))
                w=jnp.maximum(inv-r*(inv*inv),0.0)
                t_=w*s
                return (w*w)*(w*t_)*((1.25-t_)*j(3))
            def many(k,total):
                t=first+k*JB
                return total+functools.reduce(lambda p,q:p+q,[tile(t+i) for i in range(JB)])
            total=lax.fori_loop(0,nfull,many,jnp.zeros((IB,128),jnp.float32))
            if JB>1:
                total=lax.fori_loop(first+nfull*JB,last,lambda t,tt:tt+tile(t),total)
            acc[a,rows,:]=total
            return 0
        lax.fori_loop(0,(count+IB-1)//IB,iblock,0)
        return 0
    lax.fori_loop(0,CELLS,cell,0)
    for a in range(CELLS):
        sums=jnp.sum(acc[a].T,axis=0,keepdims=True)
        there=rec[a,3:4,:]>0
        rho[a:a+1,:]=jnp.where(there,(32.0*NORM)*sums,0.0)
        safe[a:a+1,:]=jnp.where(there,(32.0*NORM)*sums,1.0)

def density(rec,meta,pairs,IB=64,JB=2,approx=True):
    V=pl.BlockSpec(memory_space=pltpu.VMEM); S=pl.BlockSpec(memory_space=pltpu.SMEM)
    return pl.pallas_call(functools.partial(density_kernel,IB,JB,approx),
        out_shape=(jax.ShapeDtypeStruct((CELLS,SLOTS),jnp.float32),jax.ShapeDtypeStruct((CELLS,SLOTS),jnp.float32),jax.ShapeDtypeStruct((384,),jnp.int32),jax.ShapeDtypeStruct((MAXT,8,128),jnp.float32)),
        in_specs=[V,S,S],out_specs=(V,V,S,V),
        scratch_shapes=[pltpu.SMEM((CELLS,),jnp.int32),pltpu.SMEM((NPAIRS,),jnp.int32),pltpu.VMEM((4,SLOTS,128),jnp.float32),pltpu.VMEM((CELLS,SLOTS,128),jnp.float32)],
        compiler_params=pltpu.CompilerParams(vmem_limit_bytes=48<<20),
        name="density")(rec,meta,pairs)

def force_kernel(IB,JB,approx,rec,snd,rho,meta,tab,buf,out,extra,cells,icol,acc):
    for n in range(9):
        for half in range(2):
            c8=slice(8*half,8*half+8)
            c2=snd[n,c8,:]; rr=rho[n,c8,:]
            base=(n*16+8*half)*8
            for c in range(8):
                cells[n*16+8*half+c,0:1,:]=0.5*jnp.sqrt(c2[c:c+1])
                cells[n*16+8*half+c,1:2,:]=c2[c:c+1]/rr[c:c+1]
                cells[n*16+8*half+c,2:3,:]=rr[c:c+1]
    lane=lax.broadcasted_iota(jnp.int32,(8,128),1)
    def put(k,_):
        src=tab[k]
        append(extra,cells[src,:,0:128],cells[src,:,128:256],tab[NPAIRS+k],lane)
        return 0
    lax.fori_loop(0,NPAIRS,put,0,unroll=2)
    def cell(a,_):
        cols=rec[a].T; more=cells[a].T
        for f,rw in enumerate((0,1,2,4,5,6,7)):
            icol[f]=jnp.broadcast_to(cols[:,rw:rw+1],(SLOTS,128))
        for f in range(3):
            icol[7+f]=jnp.broadcast_to(more[:,f:f+1],(SLOTS,128))
        first=tab[FIRST+a]; last=tab[FIRST+a+1]
        nfull=(last-first)//JB
        count=meta[a]
        def iblock(g,_):
            rows=pl.ds(pl.multiple_of(g*IB,IB),IB)
            def tile(t):
                i=lambda f: icol[f,rows,:]
                j=lambda rw: buf[t,rw:rw+1,:]
                e=lambda rw: extra[t,rw:rw+1,:]
                dx=i(0)-j(0); dy=i(1)-j(1); dz=i(2)-j(2)
                r2=dx*dx+dy*dy+dz*dz
                s=i(3)+j(4)
                inv=rcp(s,approx)
                r=r2*lax.rsqrt(jnp.maximum(r2,1e-30))
                i2=inv*inv
                w=jnp.maximum(inv-r*i2,0.0)
                va=jnp.minimum((i(4)-j(5))*dx+(i(5)-j(6))*dy+(i(6)-j(7))*dz,0.0)
                m=s*va*rcp(r2+0.0025*(s*s),approx)
                visc=m*((m-i(7))-e(0))*rcp(i(9)+e(2),approx)
                f=(i(8)+e(1)+visc)*j(3)*((w*w)*(w*i2))
                return f*dx,f*dy,f*dz
            def many(k,total):
                t=first+k*JB
                ts=[tile(t+q) for q in range(JB)]
                return tuple(total[c]+functools.reduce(lambda p,q:p+q,[x[c] for x in ts]) for c in range(3))
            z=jnp.zeros((IB,128),jnp.float32)
            total=lax.fori_loop(0,nfull,many,(z,z,z))
            if JB>1:
                def one(t,tt):
                    x=tile(t)
                    return tuple(p+q for p,q in zip(tt,x))
                total=lax.fori_loop(first+nfull*JB,last,one,total)
            for c in range(3):
                acc[c,a,rows,:]=total[c]
            return 0
        lax.fori_loop(0,(count+IB-1)//IB,iblock,0)
        return 0
    lax.fori_loop(0,CELLS,cell,0)
    for a in range(CELLS):
        for c in range(3):
            sums=jnp.sum(acc[c,a].T,axis=0,keepdims=True)
            out[c,a:a+1,:]=jnp.where(rec[a,3:4,:]>0,(160.0*NORM)*sums,0.0)

def force(rec,snd,rho,meta,tab,buf,IB=32,JB=2,approx=True):
    V=pl.BlockSpec(memory_space=pltpu.VMEM); S=pl.BlockSpec(memory_space=pltpu.SMEM)
    return pl.pallas_call(functools.partial(force_kernel,IB,JB,approx),
        out_shape=jax.ShapeDtypeStruct((3,CELLS,SLOTS),jnp.float32),
        in_specs=[V,V,V,S,S,V],out_specs=V,
        scratch_shapes=[pltpu.VMEM((MAXT,8,128),jnp.float32),pltpu.VMEM((144,8,SLOTS),jnp.float32),pltpu.VMEM((10,SLOTS,128),jnp.float32),pltpu.VMEM((3,CELLS,SLOTS,128),jnp.float32)],
        compiler_params=pltpu.CompilerParams(vmem_limit_bytes=48<<20),
        name="force")(rec,snd,rho,meta,tab,buf)


from jax.sharding import PartitionSpec as P

N_GX=16; N_GY=8
AROUND=((-1,-1),(-1,0),(-1,1),(0,-1),(0,1),(1,-1),(1,0),(1,1))
MESH=pl.DeviceIdType.MESH


def neighbours(u, w):
    return [(lax.rem(u + du + N_GX, N_GX), lax.rem(w + dw + N_GY, N_GY)) for du, dw in AROUND]


def exchange_kernel(pos, vel, mass, smooth, snd, counts, move, lists, rec_out, snd_out, meta_out,
                    rec, outbox, inbox, metas, send1, recv1, send2, recv2):
    u, w = lax.axis_index("gx"), lax.axis_index("gy")
    around = neighbours(u, w)
    barrier = pltpu.get_barrier_semaphore()
    for off in range(1, N_GX):
        pl.semaphore_signal(barrier, inc=1, device_id=(lax.rem(u + off, N_GX), w), device_id_type=MESH)
    for n, (du, dw) in enumerate(AROUND):
        if dw != 0:
            pl.semaphore_signal(barrier, inc=1, device_id=around[n], device_id_type=MESH)

    slot = lax.broadcasted_iota(jnp.int32, (1, 256), 1)
    for c in range(16):
        for f in range(3):
            rec[c, f:f + 1, :] = pos[f, c:c + 1, :]
            rec[c, 5 + f:6 + f, :] = vel[f, c:c + 1, :]
        rec[c, 3:4, :] = jnp.where(slot < counts[c], mass[c:c + 1, :], 0.0)
        rec[c, 4:5, :] = smooth[c:c + 1, :]

    columns = [lax.shift_right_logical(move[c], 7) for c in range(16)]
    row = lax.broadcasted_iota(jnp.int32, (8, 256), 0)

    def post(off, _):
        column = lax.rem(u + off, N_GX)
        first, last = jnp.int32(16), jnp.int32(-1)
        for c in range(16):
            match = columns[c] == column
            first = jnp.minimum(first, jnp.where(match, c, 16))
            last = jnp.where(match, c, last)
        found = last >= 0
        first = jnp.where(found, first, 0)
        last = jnp.where(found, last, 0)
        outbox[off, 0:8, :] = rec[first]
        outbox[off, 8:16, :] = rec[last]
        number = lambda c: jnp.where(found, move[c], -1).astype(jnp.float32)
        amount = lambda c: counts[c].astype(jnp.float32)
        more = jnp.where(row == 0, snd[pl.ds(first, 1), :], snd[pl.ds(last, 1), :])
        more = jnp.where(row == 2, number(first), more)
        more = jnp.where(row == 3, number(last), more)
        more = jnp.where(row == 4, amount(first), more)
        more = jnp.where(row == 5, amount(last), more)
        outbox[off, 16:24, :] = more
        return 0

    lax.fori_loop(0, N_GX, post, 0)
    pl.semaphore_wait(barrier, N_GX - 1 + 6)

    def parcel(off):
        return pltpu.make_async_remote_copy(
            src_ref=outbox.at[off], dst_ref=inbox.at[off], send_sem=send1.at[off], recv_sem=recv1.at[off],
            device_id=(lax.rem(u + off, N_GX), w), device_id_type=MESH)

    def start(off, _):
        parcel(off).start()
        return 0

    lax.fori_loop(1, N_GX, start, 0)
    inbox[0] = outbox[0]

    first_own = ((u * N_GY + w) * 16).astype(jnp.float32)
    sub = lax.broadcasted_iota(jnp.int32, (16, 256), 0).astype(jnp.float32) + first_own
    lane = lax.broadcasted_iota(jnp.int32, (1, 128), 1).astype(jnp.float32) + first_own

    def absorb(off, carry):
        cells, sounds, amounts = carry
        cells = list(cells)
        for k in range(2):
            block = inbox[off, 8 * k:8 * k + 8, :]
            sound = inbox[off, 16 + k:17 + k, :]
            number = inbox[off, 18 + k:19 + k, :]
            amount = inbox[off, 20 + k:21 + k, 0:128]
            sounds = jnp.where(sub == number, sound, sounds)
            amounts = jnp.where(lane == number[:, 0:128], amount, amounts)
            wide = jnp.broadcast_to(number, (8, 256))
            for t in range(16):
                cells[t] = jnp.where(wide == first_own + t, block, cells[t])
        return tuple(cells), sounds, amounts

    def absorb_next(off, carry):
        parcel(off).wait_recv()
        return absorb(off, carry)

    zero = jnp.zeros((8, 256), jnp.float32)
    carry = absorb(0, ((zero,) * 16, jnp.zeros((16, 256), jnp.float32), jnp.zeros((1, 128), jnp.float32)))
    cells, sounds, amounts = lax.fori_loop(1, N_GX, absorb_next, carry)
    for t in range(16):
        rec_out[0, t] = cells[t]
    snd_out[0] = sounds
    amounts = amounts.astype(jnp.int32)
    slot = lax.broadcasted_iota(jnp.int32, (1, 128), 1)
    meta_out[0] = amounts
    for n in range(8):
        metas[n] = jnp.where(slot < 16, amounts, lists[n:n + 1, :])

    copies = []
    for n in range(8):
        for k, (src, dst) in enumerate(((metas.at[n], meta_out.at[n + 1]), (rec_out.at[0], rec_out.at[n + 1]), (snd_out.at[0], snd_out.at[n + 1]))):
            copy = pltpu.make_async_remote_copy(
                src_ref=src, dst_ref=dst, send_sem=send2.at[n, k], recv_sem=recv2.at[n, k],
                device_id=around[n], device_id_type=MESH)
            copy.start()
            copies.append(copy)

    def sent(off, _):
        parcel(off).wait_send()
        return 0

    lax.fori_loop(1, N_GX, sent, 0)
    for copy in copies:
        copy.wait()


VMEM=pl.BlockSpec(memory_space=pltpu.VMEM)
SMEM=pl.BlockSpec(memory_space=pltpu.SMEM)

def exchange(positions, velocities, masses, smoothing, sound2, counts, move_to, lists):
    return pl.pallas_call(
        exchange_kernel,
        out_shape=(jax.ShapeDtypeStruct((9, 16, 8, 256), jnp.float32),
                   jax.ShapeDtypeStruct((9, 16, 256), jnp.float32),
                   jax.ShapeDtypeStruct((9, 1, 128), jnp.int32)),
        in_specs=[VMEM] * 5 + [SMEM] * 2 + [VMEM],
        out_specs=(VMEM,) * 3,
        scratch_shapes=[
            pltpu.VMEM((16, 8, 256), jnp.float32),
            pltpu.VMEM((N_GX, 24, 256), jnp.float32),
            pltpu.VMEM((N_GX, 24, 256), jnp.float32),
            pltpu.VMEM((8, 1, 128), jnp.int32),
            pltpu.SemaphoreType.DMA((N_GX,)),
            pltpu.SemaphoreType.DMA((N_GX,)),
            pltpu.SemaphoreType.DMA((8, 3)),
            pltpu.SemaphoreType.DMA((8, 3)),
        ],
        compiler_params=pltpu.CompilerParams(collective_id=0, has_side_effects=True, vmem_limit_bytes=32 << 20),
        name="exchange",
    )(positions, velocities, masses, smoothing, sound2, counts, move_to, lists)


def share_kernel(own, out, send, recv):
    u, w = lax.axis_index("gx"), lax.axis_index("gy")
    around = neighbours(u, w)
    barrier = pltpu.get_barrier_semaphore()
    for n in range(8):
        pl.semaphore_signal(barrier, inc=1, device_id=around[n], device_id_type=MESH)
    pl.semaphore_wait(barrier, 8)
    copies = []
    for n in range(8):
        copy = pltpu.make_async_remote_copy(
            src_ref=own, dst_ref=out.at[n + 1], send_sem=send.at[n], recv_sem=recv.at[n],
            device_id=around[n], device_id_type=MESH)
        copy.start()
        copies.append(copy)
    out[0] = own[...]
    for copy in copies:
        copy.wait()


def share(own):
    return pl.pallas_call(
        share_kernel,
        out_shape=jax.ShapeDtypeStruct((9, 16, 256), jnp.float32),
        in_specs=[VMEM], out_specs=VMEM,
        scratch_shapes=[pltpu.SemaphoreType.DMA((8,)), pltpu.SemaphoreType.DMA((8,))],
        compiler_params=pltpu.CompilerParams(collective_id=1, has_side_effects=True),
        name="share",
    )(own)


def body(positions, velocities, masses, smoothing, sound2, counts, move_to, proxy_send, pairs):
    lists = jnp.pad(proxy_send.reshape(8, 16), ((0, 0), (16, 96)))
    rec, snd, meta = exchange(positions, velocities, masses, smoothing, sound2, counts, move_to, lists)
    rec = rec.reshape(144, 8, 256)
    meta = meta.reshape(-1)
    rho, safe, tab, buf = density(rec, meta, pairs.reshape(-1))
    rho_all = share(safe)
    accel = force(rec, snd, rho_all, meta, tab, buf)
    return rho, accel


def solution(mesh):
    flat, cells, three = P(("gx", "gy")), P(("gx", "gy"), None), P(None, ("gx", "gy"), None)
    return jax.shard_map(
        body, mesh=mesh,
        in_specs=(three, three, cells, cells, cells, flat, flat, flat, cells),
        out_specs=(cells, three), check_vma=False)
```

time: 362 us -> 154 us (0.43)
  the two profiles are of different devices: /device:TPU:0 before, /device:TPU:6 now
where the time goes in v1:
time: 154 us
  Pallas kernels  144 us (94%)
  local copies, waits for them, and re-layouts  8.36 us (5%)
    pallas_call x1, Pallas kernels, force(): pl.pallas_call(functools.partial(force_kernel, IB, JB, approx), out_shape...  62.9 us
    pallas_call x1, Pallas kernels, density(): pl.pallas_call(functools.partial(density_kernel, IB, JB, approx), out_sha...  44 us
    pallas_call x1, Pallas kernels, exchange(): pl.pallas_call(exchange_kernel, out_shape=(jax.ShapeDtypeStruct((9, 16, 8...  27.8 us
    pallas_call x1, Pallas kernels, share(): pl.pallas_call(share_kernel, out_shape=jax.ShapeDtypeStruct((9, 16, 256),...  9.71 us
    unnamed x19, local copies, waits for them, and re-layouts  7.35 us

profile of v1, /device:TPU:6, one launch (start us, length us, event | category | flops | bytes accessed | tf_op | source)
XLA Modules:
  0.0 153.5 jit_solution(2448221912741025639)
XLA Ops:
  0.6 0.7 reshape.16
  1.4 0.1 pad.4.lists
  1.4 0.8 copy.11
  2.2 0.2 reshape.19.pairs
  2.4 0.0 copy-start.1
  2.5 0.8 copy-done.1
  3.3 0.0 copy-start.2
  3.3 0.8 copy-done.2
  4.0 0.0 copy-start.3
  4.1 0.7 copy-done.3
  4.8 0.0 copy-start.4
  4.8 0.7 copy-done.4
  5.5 0.0 copy-start.5
  5.5 0.7 copy-done.5
  6.2 0.0 copy-start.7
  6.2 0.7 copy-done.7
  6.9 0.0 copy-start.8
  6.9 0.7 copy-done.8
  7.5 27.8 %exchange.1 = (f32[9,16,8,256]{3,2,1,0:T(8,128)S(1)}, f32[9,16,256]{2,1,0:T(8,128)S(1)}, s32[9,1,128]{2,1,0:T(1,128)S(1)}) custom-call(f32[3,16,256]{2,1,0:T(8,128)S(1)} %copy-done.1, f32[3,16,256]{2,1,0:T(8,128)S(1)} %copy-done.2, f32[16,256]{1,0:T(8,128)S(1)} %copy-done.3, f32[16,256]{1,0:T(8,128)S(1)} %copy-done.4, f32[16,256]{1,0:T(8,128)S(1)} %copy-done.5, ...), custom_call_target="tpu_custom_call" | custom-call | tf_op jit(solution)/shard_map/exchange/pallas_call | solution.py:312
  35.3 44.0 %density.1 = (f32[16,256]{1,0:T(8,128)}, f32[16,256]{1,0:T(8,128)S(1)}, s32[384]{0:T(512)S(1)}, f32[344,8,128]{2,1,0:T(8,128)S(1)}) custom-call(f32[144,8,256]{2,1,0:T(8,128)S(1)} %bitcast.2, s32[1152]{0:T(1024)S(1)} %bitcast.4, s32[480]{0:T(512)S(1)} %reshape.19.pairs), custom_call_target="tpu_custom_call" | custom-call | tf_op jit(solution)/shard_map/density/pallas_call | solution.py:103
  79.4 0.0 copy-start.6
  79.4 0.6 copy-done.6
  80.0 9.7 %share.1.rho = f32[9,16,256]{2,1,0:T(8,128)} custom-call(f32[16,256]{1,0:T(8,128)} %copy-done.6), custom_call_target="tpu_custom_call" | custom-call | tf_op jit(solution)/shard_map/share/pallas_call | solution.py:354
  89.7 0.0 copy-start
  89.7 0.9 copy-done
  90.6 62.9 %force.1 = f32[3,16,256]{2,1,0:T(8,128)} custom-call(f32[144,8,256]{2,1,0:T(8,128)S(1)} %bitcast.3, f32[9,16,256]{2,1,0:T(8,128)S(1)} %get-tuple-element.12.snd, f32[9,16,256]{2,1,0:T(8,128)S(1)} %copy-done, s32[1152]{0:T(1024)S(1)} %bitcast.5, s32[384]{0:T(512)S(1)} %get-tuple-element.14.tab, f32[344,8,128]{2,1,0:T(8,128)S(1)} %get-tuple-element.15.buf), custom_call_target="tpu_custom_call" | custom-call | tf_op jit(solution)/shard_map/force/pallas_call | solution.py:177
  (1 shorter events, 0.0 us)
Async XLA Ops:
  2.4 0.8 copy-start.1
  3.3 0.8 copy-start.2
  4.0 0.7 copy-start.3
  4.8 0.7 copy-start.4
  5.5 0.7 copy-start.5
  6.2 0.7 copy-start.7
  6.9 0.7 copy-start.8
  79.4 0.6 copy-start.6
  89.7 0.9 copy-start

commit v2 on v1

v2 whole, which is shorter than its diff:
```python
import math, functools
import jax, jax.numpy as jnp
from jax import lax
from jax.experimental import pallas as pl
from jax.experimental.pallas import tpu as pltpu

CELLS=16; SLOTS=256; NPAIRS=160; NORM=21.0/(16.0*math.pi)
WHOLE=63<<20
MAXT=2*NPAIRS+3*CELLS+8
PLACE=NPAIRS; FIRST=2*NPAIRS; LAST=FIRST+CELLS

def rcp(x):
    return pl.reciprocal(x, approx=True)

def append(buf, x0, x1, pos, lane):
    tile=lax.shift_right_logical(pos,7); s=lax.bitwise_and(pos,127)
    t0=pltpu.roll(x0,s,1); t1=pltpu.roll(x1,s,1)
    keep=lane>=s
    pltpu.store(buf.at[tile],t0,mask=keep)
    buf[tile+1]=jnp.where(keep,t1,t0)
    buf[tile+2]=jnp.where(keep,0.0,t1)

def plan(meta, pairs, tab, filled, count_of):
    for a in range(CELLS):
        filled[a]=0
    def size(p,_):
        a=pairs[0,p]; b=pairs[1,p]
        n=lax.shift_right_logical(b,4); r=lax.bitwise_and(b,15)
        cell=jnp.where(n==0,r,meta[n,1,jnp.maximum(n-1,0)*16+r])
        count=meta[n,0,cell]
        tab[p]=n*16+cell
        count_of[p]=count
        filled[a]=filled[a]+count
        return 0
    lax.fori_loop(0,NPAIRS,size,0,unroll=8)
    tile=jnp.int32(0)
    for a in range(CELLS):
        end=tile+lax.shift_right_logical(filled[a]+127,7)
        tab[FIRST+a]=tile; tab[LAST+a]=end
        filled[a]=tile*128
        tile=end+2

def pack_main(rec, pairs, tab, filled, count_of, shifts, buf, unroll):
    lane=lax.broadcasted_iota(jnp.int32,(8,128),1)
    row=lax.broadcasted_iota(jnp.int32,(8,128),0)
    for d in range(27):
        dx,dy,dz=d//9-1,d//3%3-1,d%3-1
        shifts[d]=jnp.where(row==0,float(dx),jnp.where(row==1,float(dy),jnp.where(row==2,float(dz),0.0)))
    def put(p,_):
        a=pairs[0,p]
        pos=filled[a]
        filled[a]=pos+count_of[p]
        tab[PLACE+p]=pos
        src=tab[p]; shift=shifts[pairs[2,p]]
        append(buf,rec[src,:,0:128]+shift,rec[src,:,128:256]+shift,pos,lane)
        return 0
    lax.fori_loop(0,NPAIRS,put,0,unroll=unroll)

def spread(icol, f, row):
    for half in range(2):
        part=slice(128*half,128*half+128)
        icol[f,part,:]=jnp.broadcast_to(row[:,part],(128,128)).T

def fetch(pairs_of_refs, sems):
    copies=[pltpu.make_async_copy(src,dst,sems.at[k]) for k,(src,dst) in enumerate(pairs_of_refs)]
    for copy in copies:
        copy.start()
    return copies

def density_kernel(IB,JB,U,rec_in,meta_in,pairs_in,rho,safe,tab,buf_out,rec,meta,pairs,buf,sems,filled,count_of,shifts,icol,acc):
    copies=fetch(((meta_in,meta),(pairs_in,pairs),(rec_in,rec)),sems)
    copies[0].wait(); copies[1].wait()
    plan(meta,pairs,tab,filled,count_of)
    copies[2].wait()
    pack_main(rec,pairs,tab,filled,count_of,shifts,buf,U)
    leave=pltpu.make_async_copy(buf,buf_out,sems.at[3])
    leave.start()
    def cell(a,_):
        for f,rw in enumerate((0,1,2,4)):
            spread(icol,f,rec[a,rw:rw+1,:])
        first=tab[FIRST+a]; last=tab[LAST+a]
        nfull=(last-first)//JB
        count=meta[0,0,a]
        def iblock(g,_):
            rows=pl.ds(pl.multiple_of(g*IB,IB),IB)
            xi,yi,zi,hi=(icol[f,rows,:] for f in range(4))
            def tile(t):
                j=lambda rw: buf[t,rw:rw+1,:]
                dx=xi-j(0); dy=yi-j(1); dz=zi-j(2)
                r2=dx*dx+dy*dy+dz*dz
                s=hi+j(4)
                inv=rcp(s)
                r=r2*lax.rsqrt(jnp.maximum(r2,1e-30))
                w=jnp.maximum(inv-r*(inv*inv),0.0)
                t_=w*s
                return (w*w)*(w*t_)*((1.25-t_)*j(3))
            def many(k,total):
                t=first+k*JB
                return total+functools.reduce(lambda p,q:p+q,[tile(t+i) for i in range(JB)])
            total=lax.fori_loop(0,nfull,many,jnp.zeros((IB,128),jnp.float32))
            if JB>1:
                total=lax.fori_loop(first+nfull*JB,last,lambda t,tt:tt+tile(t),total)
            acc[a,rows,:]=total
            return 0
        lax.fori_loop(0,(count+IB-1)//IB,iblock,0)
        return 0
    lax.fori_loop(0,CELLS,cell,0)
    for a in range(CELLS):
        sums=jnp.sum(acc[a].T,axis=0,keepdims=True)
        there=rec[a,3:4,:]>0
        rho[a:a+1,:]=jnp.where(there,(32.0*NORM)*sums,0.0)
        safe[a:a+1,:]=jnp.where(there,(32.0*NORM)*sums,1.0)
    leave.wait()

def density(rec,meta,pairs,IB=64,JB=2,U=8):
    V=pl.BlockSpec(memory_space=pltpu.VMEM); S=pl.BlockSpec(memory_space=pltpu.SMEM); H=pl.BlockSpec(memory_space=pltpu.HBM)
    return pl.pallas_call(functools.partial(density_kernel,IB,JB,U),
        out_shape=(jax.ShapeDtypeStruct((CELLS,SLOTS),jnp.float32),jax.ShapeDtypeStruct((CELLS,SLOTS),jnp.float32),jax.ShapeDtypeStruct((384,),jnp.int32),jax.ShapeDtypeStruct((MAXT,8,128),jnp.float32)),
        in_specs=[H,H,H],out_specs=(V,V,S,H),
        scratch_shapes=[pltpu.VMEM((144,8,SLOTS),jnp.float32),pltpu.SMEM((9,2,128),jnp.int32),pltpu.SMEM((3,NPAIRS),jnp.int32),pltpu.VMEM((MAXT,8,128),jnp.float32),pltpu.SemaphoreType.DMA((4,)),pltpu.SMEM((CELLS,),jnp.int32),pltpu.SMEM((NPAIRS,),jnp.int32),pltpu.VMEM((27,8,128),jnp.float32),pltpu.VMEM((4,SLOTS,128),jnp.float32),pltpu.VMEM((CELLS,SLOTS,128),jnp.float32)],
        compiler_params=pltpu.CompilerParams(vmem_limit_bytes=WHOLE),
        name="density")(rec,meta,pairs)

def force_kernel(IB,JB,U,rec_in,snd_in,rho_in,meta_in,tab_in,buf_in,out,rec,snd,rho,meta,tab,buf,sems,extra,cells,icol,acc):
    copies=fetch(((snd_in,snd),(rho_in,rho),(tab_in,tab),(meta_in.at[0],meta.at[0]),(rec_in.at[pl.ds(0,CELLS)],rec),(buf_in,buf)),sems)
    for copy in copies[:4]:
        copy.wait()
    for n in range(9):
        for half in range(2):
            c8=slice(8*half,8*half+8)
            c2=snd[n,c8,:]; rr=rho[n,c8,:]
            base=(n*16+8*half)*8
            for f,val in enumerate((0.5*(c2*lax.rsqrt(c2)),c2*rcp(rr),rr)):
                cells[0,pl.ds(base+f,8,stride=8),:]=val[:,0:128]
                cells[1,pl.ds(base+f,8,stride=8),:]=val[:,128:256]
    lane=lax.broadcasted_iota(jnp.int32,(8,128),1)
    block=lambda src: pl.ds(pl.multiple_of(src*8,8),8)
    def put(p,_):
        src=tab[p]
        append(extra,cells[0,block(src),:],cells[1,block(src),:],tab[PLACE+p],lane)
        return 0
    lax.fori_loop(0,NPAIRS,put,0,unroll=U)
    for copy in copies[4:]:
        copy.wait()
    def cell(a,_):
        for f,rw in enumerate((0,1,2,4,5,6,7)):
            spread(icol,f,rec[a,rw:rw+1,:])
        for f in range(3):
            for half in range(2):
                icol[7+f,128*half:128*half+128,:]=jnp.broadcast_to(cells[half,pl.ds(a*8+f,1),:],(128,128)).T
        first=tab[FIRST+a]; last=tab[LAST+a]
        nfull=(last-first)//JB
        count=meta[0,0,a]
        def iblock(g,_):
            rows=pl.ds(pl.multiple_of(g*IB,IB),IB)
            def tile(t):
                i=lambda f: icol[f,rows,:]
                j=lambda rw: buf[t,rw:rw+1,:]
                e=lambda rw: extra[t,rw:rw+1,:]
                dx=i(0)-j(0); dy=i(1)-j(1); dz=i(2)-j(2)
                r2=dx*dx+dy*dy+dz*dz
                s=i(3)+j(4)
                inv=rcp(s)
                r=r2*lax.rsqrt(jnp.maximum(r2,1e-30))
                i2=inv*inv
                w=jnp.maximum(inv-r*i2,0.0)
                va=jnp.minimum((i(4)-j(5))*dx+(i(5)-j(6))*dy+(i(6)-j(7))*dz,0.0)
                m=s*va*rcp(r2+0.0025*(s*s))
                visc=m*((m-i(7))-e(0))*rcp(i(9)+e(2))
                f=(i(8)+e(1)+visc)*j(3)*((w*w)*(w*i2))
                return f*dx,f*dy,f*dz
            def many(k,total):
                t=first+k*JB
                ts=[tile(t+q) for q in range(JB)]
                return tuple(total[c]+functools.reduce(lambda p,q:p+q,[x[c] for x in ts]) for c in range(3))
            z=jnp.zeros((IB,128),jnp.float32)
            total=lax.fori_loop(0,nfull,many,(z,z,z))
            if JB>1:
                def one(t,tt):
                    x=tile(t)
                    return tuple(p+q for p,q in zip(tt,x))
                total=lax.fori_loop(first+nfull*JB,last,one,total)
            for c in range(3):
                acc[c,a,rows,:]=total[c]
            return 0
        lax.fori_loop(0,(count+IB-1)//IB,iblock,0)
        return 0
    lax.fori_loop(0,CELLS,cell,0)
    for a in range(CELLS):
        for c in range(3):
            sums=jnp.sum(acc[c,a].T,axis=0,keepdims=True)
            out[c,a:a+1,:]=jnp.where(rec[a,3:4,:]>0,(160.0*NORM)*sums,0.0)

def force(rec,snd,rho,meta,tab,buf,IB=32,JB=2,U=8):
    V=pl.BlockSpec(memory_space=pltpu.VMEM); S=pl.BlockSpec(memory_space=pltpu.SMEM); H=pl.BlockSpec(memory_space=pltpu.HBM)
    return pl.pallas_call(functools.partial(force_kernel,IB,JB,U),
        out_shape=jax.ShapeDtypeStruct((3,CELLS,SLOTS),jnp.float32),
        in_specs=[H]*6,out_specs=V,
        scratch_shapes=[pltpu.VMEM((CELLS,8,SLOTS),jnp.float32),pltpu.VMEM((9,CELLS,SLOTS),jnp.float32),pltpu.VMEM((9,CELLS,SLOTS),jnp.float32),pltpu.SMEM((1,2,128),jnp.int32),pltpu.SMEM((384,),jnp.int32),pltpu.VMEM((MAXT,8,128),jnp.float32),pltpu.SemaphoreType.DMA((6,)),pltpu.VMEM((MAXT,8,128),jnp.float32),pltpu.VMEM((2,144*8,128),jnp.float32),pltpu.VMEM((10,SLOTS,128),jnp.float32),pltpu.VMEM((3,CELLS,SLOTS,128),jnp.float32)],
        compiler_params=pltpu.CompilerParams(vmem_limit_bytes=WHOLE),
        name="force")(rec,snd,rho,meta,tab,buf)


from jax.sharding import PartitionSpec as P

N_GX=16; N_GY=8
AROUND=((-1,-1),(-1,0),(-1,1),(0,-1),(0,1),(1,-1),(1,0),(1,1))
MESH=pl.DeviceIdType.MESH


def neighbours(u, w):
    return [(lax.rem(u + du + N_GX, N_GX), lax.rem(w + dw + N_GY, N_GY)) for du, dw in AROUND]


def exchange_kernel(*refs):
    given, (rec_out, snd_out, meta_out), scratch = refs[:8], refs[8:11], refs[11:]
    held, (rec, outbox, inbox, metas, moved, sounds_moved, load, send1, recv1, send2, recv2) = scratch[:8], scratch[8:]
    pos, vel, mass, smooth, snd, counts, move, lists = held
    u, w = lax.axis_index("gx"), lax.axis_index("gy")
    loads = [pltpu.make_async_copy(src, dst, load.at[k]) for k, (src, dst) in enumerate(zip(given, held))]
    for copy in loads:
        copy.start()
    around = neighbours(u, w)
    barrier = pltpu.get_barrier_semaphore()
    for off in range(1, N_GX):
        pl.semaphore_signal(barrier, inc=1, device_id=(lax.rem(u + off, N_GX), w), device_id_type=MESH)
    for n, (du, dw) in enumerate(AROUND):
        if dw != 0:
            pl.semaphore_signal(barrier, inc=1, device_id=around[n], device_id_type=MESH)

    for copy in loads:
        copy.wait()
    slot = lax.broadcasted_iota(jnp.int32, (1, 256), 1)
    for c in range(16):
        for f in range(3):
            rec[c, f:f + 1, :] = pos[f, c:c + 1, :]
            rec[c, 5 + f:6 + f, :] = vel[f, c:c + 1, :]
        rec[c, 3:4, :] = jnp.where(slot < counts[c], mass[c:c + 1, :], 0.0)
        rec[c, 4:5, :] = smooth[c:c + 1, :]

    columns = [lax.shift_right_logical(move[c], 7) for c in range(16)]
    row = lax.broadcasted_iota(jnp.int32, (8, 256), 0)

    def post(off, _):
        column = lax.rem(u + off, N_GX)
        first, last = jnp.int32(16), jnp.int32(-1)
        for c in range(16):
            match = columns[c] == column
            first = jnp.minimum(first, jnp.where(match, c, 16))
            last = jnp.where(match, c, last)
        found = last >= 0
        first = jnp.where(found, first, 0)
        last = jnp.where(found, last, 0)
        outbox[off, 0:8, :] = rec[first]
        outbox[off, 8:16, :] = rec[last]
        number = lambda c: jnp.where(found, move[c], -1).astype(jnp.float32)
        amount = lambda c: counts[c].astype(jnp.float32)
        more = jnp.where(row == 0, snd[pl.ds(first, 1), :], snd[pl.ds(last, 1), :])
        more = jnp.where(row == 2, number(first), more)
        more = jnp.where(row == 3, number(last), more)
        more = jnp.where(row == 4, amount(first), more)
        more = jnp.where(row == 5, amount(last), more)
        outbox[off, 16:24, :] = more
        return 0

    lax.fori_loop(0, N_GX, post, 0)
    pl.semaphore_wait(barrier, N_GX - 1 + 6)

    def parcel(off):
        return pltpu.make_async_remote_copy(
            src_ref=outbox.at[off], dst_ref=inbox.at[off], send_sem=send1.at[off], recv_sem=recv1.at[off],
            device_id=(lax.rem(u + off, N_GX), w), device_id_type=MESH)

    def start(off, _):
        parcel(off).start()
        return 0

    lax.fori_loop(1, N_GX, start, 0)
    inbox[0] = outbox[0]

    first_own = ((u * N_GY + w) * 16).astype(jnp.float32)
    sub = lax.broadcasted_iota(jnp.int32, (16, 256), 0).astype(jnp.float32) + first_own
    lane = lax.broadcasted_iota(jnp.int32, (1, 128), 1).astype(jnp.float32) + first_own

    def absorb(off, carry):
        cells, sounds, amounts = carry
        cells = list(cells)
        for k in range(2):
            block = inbox[off, 8 * k:8 * k + 8, :]
            sound = inbox[off, 16 + k:17 + k, :]
            number = inbox[off, 18 + k:19 + k, :]
            amount = inbox[off, 20 + k:21 + k, 0:128]
            sounds = jnp.where(sub == number, sound, sounds)
            amounts = jnp.where(lane == number[:, 0:128], amount, amounts)
            wide = jnp.broadcast_to(number, (8, 256))
            for t in range(16):
                cells[t] = jnp.where(wide == first_own + t, block, cells[t])
        return tuple(cells), sounds, amounts

    def absorb_next(off, carry):
        parcel(off).wait_recv()
        return absorb(off, carry)

    zero = jnp.zeros((8, 256), jnp.float32)
    carry = absorb(0, ((zero,) * 16, jnp.zeros((16, 256), jnp.float32), jnp.zeros((1, 128), jnp.float32)))
    cells, sounds, amounts = lax.fori_loop(1, N_GX, absorb_next, carry)
    for t in range(16):
        moved[t] = cells[t]
    sounds_moved[...] = sounds
    metas[0:1, :] = amounts.astype(jnp.int32)
    metas[1:2, :] = lists[...]

    copies = []
    own = ((metas, meta_out), (moved, rec_out), (sounds_moved, snd_out))
    for n in range(8):
        for k, (src, dst) in enumerate(own):
            copy = pltpu.make_async_remote_copy(
                src_ref=src, dst_ref=dst.at[n + 1], send_sem=send2.at[n, k], recv_sem=recv2.at[n, k],
                device_id=around[n], device_id_type=MESH)
            copy.start()
            copies.append(copy)
    for k, (src, dst) in enumerate(own):
        copy = pltpu.make_async_copy(src, dst.at[0], load.at[k])
        copy.start()
        copies.append(copy)

    def sent(off, _):
        parcel(off).wait_send()
        return 0

    lax.fori_loop(1, N_GX, sent, 0)
    for copy in copies:
        copy.wait()


VMEM=pl.BlockSpec(memory_space=pltpu.VMEM)
HBM=pl.BlockSpec(memory_space=pltpu.HBM)

def exchange(positions, velocities, masses, smoothing, sound2, counts, move_to, lists):
    return pl.pallas_call(
        exchange_kernel,
        out_shape=(jax.ShapeDtypeStruct((9, 16, 8, 256), jnp.float32),
                   jax.ShapeDtypeStruct((9, 16, 256), jnp.float32),
                   jax.ShapeDtypeStruct((9, 2, 128), jnp.int32)),
        in_specs=[HBM] * 8,
        out_specs=(HBM,) * 3,
        scratch_shapes=[
            pltpu.VMEM((3, 16, 256), jnp.float32),
            pltpu.VMEM((3, 16, 256), jnp.float32),
            pltpu.VMEM((16, 256), jnp.float32),
            pltpu.VMEM((16, 256), jnp.float32),
            pltpu.VMEM((16, 256), jnp.float32),
            pltpu.SMEM((16,), jnp.int32),
            pltpu.SMEM((16,), jnp.int32),
            pltpu.VMEM((1, 128), jnp.int32),
            pltpu.VMEM((16, 8, 256), jnp.float32),
            pltpu.VMEM((N_GX, 24, 256), jnp.float32),
            pltpu.VMEM((N_GX, 24, 256), jnp.float32),
            pltpu.VMEM((2, 128), jnp.int32),
            pltpu.VMEM((16, 8, 256), jnp.float32),
            pltpu.VMEM((16, 256), jnp.float32),
            pltpu.SemaphoreType.DMA((8,)),
            pltpu.SemaphoreType.DMA((N_GX,)),
            pltpu.SemaphoreType.DMA((N_GX,)),
            pltpu.SemaphoreType.DMA((8, 3)),
            pltpu.SemaphoreType.DMA((8, 3)),
        ],
        compiler_params=pltpu.CompilerParams(collective_id=0, has_side_effects=True, vmem_limit_bytes=WHOLE),
        name="exchange",
    )(positions, velocities, masses, smoothing, sound2, counts, move_to, lists)


def share_kernel(own, out, load, send, recv):
    u, w = lax.axis_index("gx"), lax.axis_index("gy")
    around = neighbours(u, w)
    barrier = pltpu.get_barrier_semaphore()
    for n in range(8):
        pl.semaphore_signal(barrier, inc=1, device_id=around[n], device_id_type=MESH)
    copies = [pltpu.make_async_copy(own, out.at[0], load)]
    copies[0].start()
    pl.semaphore_wait(barrier, 8)
    for n in range(8):
        copy = pltpu.make_async_remote_copy(
            src_ref=own, dst_ref=out.at[n + 1], send_sem=send.at[n], recv_sem=recv.at[n],
            device_id=around[n], device_id_type=MESH)
        copy.start()
        copies.append(copy)
    for copy in copies:
        copy.wait()


def share(own):
    return pl.pallas_call(
        share_kernel,
        out_shape=jax.ShapeDtypeStruct((9, 16, 256), jnp.float32),
        in_specs=[HBM], out_specs=HBM,
        scratch_shapes=[pltpu.SemaphoreType.DMA, pltpu.SemaphoreType.DMA((8,)), pltpu.SemaphoreType.DMA((8,))],
        compiler_params=pltpu.CompilerParams(collective_id=1, has_side_effects=True, vmem_limit_bytes=WHOLE),
        name="share",
    )(own)


def body(positions, velocities, masses, smoothing, sound2, counts, move_to, proxy_send, pairs):
    rec, snd, meta = exchange(positions, velocities, masses, smoothing, sound2, counts, move_to, proxy_send.reshape(1, 128))
    rec = rec.reshape(144, 8, 256)
    rho, safe, tab, buf = density(rec, meta, pairs.T)
    rho_all = share(safe)
    accel = force(rec, snd, rho_all, meta, tab, buf)
    return rho, accel


def solution(mesh):
    flat, cells, three = P(("gx", "gy")), P(("gx", "gy"), None), P(None, ("gx", "gy"), None)
    return jax.shard_map(
        body, mesh=mesh,
        in_specs=(three, three, cells, cells, cells, flat, flat, flat, cells),
        out_specs=(cells, three), check_vma=False)
```

time: 154 us -> 129 us (0.84)
  the two profiles are of different devices: /device:TPU:6 before, /device:TPU:25 now
where the time goes in v2:
time: 129 us
  Pallas kernels  128 us (99%)
    pallas_call x1, Pallas kernels, force(): pl.pallas_call(functools.partial(force_kernel, IB, JB, U), out_shape=jax....  57.4 us
    pallas_call x1, Pallas kernels, density(): pl.pallas_call(functools.partial(density_kernel, IB, JB, U), out_shape=(j...  32.9 us
    pallas_call x1, Pallas kernels, exchange(): pl.pallas_call(exchange_kernel, out_shape=(jax.ShapeDtypeStruct((9, 16, 8...  28.4 us
    pallas_call x1, Pallas kernels, share(): pl.pallas_call(share_kernel, out_shape=jax.ShapeDtypeStruct((9, 16, 256),...  9.31 us

profile of v2, /device:TPU:25, one launch (start us, length us, event | category | flops | bytes accessed | tf_op | source)
XLA Modules:
  0.0 128.7 jit_solution(2317222400596337029)
XLA Ops:
  0.6 28.4 %exchange.1 = (f32[9,16,8,256]{3,2,1,0:T(8,128)}, f32[9,16,256]{2,1,0:T(8,128)}, s32[9,2,128]{2,1,0:T(2,128)}) custom-call(f32[3,16,256]{2,1,0:T(8,128)} %refs_0_.1, f32[3,16,256]{2,1,0:T(8,128)} %refs_1_.1, f32[16,256]{1,0:T(8,128)} %refs_2_.1, f32[16,256]{1,0:T(8,128)} %refs_3_.1, f32[16,256]{1,0:T(8,128)} %refs_4_.1, s32[16]{0:T(128)} %refs_5_.1, ...), custom_call_target="tpu_custom_call" | custom-call | tf_op jit(solution)/shard_map/exchange/pallas_call | solution.py:340
  29.1 32.9 %density.1 = (f32[16,256]{1,0:T(8,128)}, f32[16,256]{1,0:T(8,128)}, s32[384]{0:T(512)}, f32[376,8,128]{2,1,0:T(8,128)}) custom-call(f32[144,8,256]{2,1,0:T(8,128)} %bitcast.3, s32[9,2,128]{2,1,0:T(2,128)} %get-tuple-element.10.meta_in, s32[3,160]{1,0:T(4,128)} %bitcast.5), custom_call_target="tpu_custom_call" | custom-call | tf_op jit(solution)/shard_map/density/pallas_call | solution.py:117
  62.0 9.3 %share.1.rho_in = f32[9,16,256]{2,1,0:T(8,128)} custom-call(f32[16,256]{1,0:T(8,128)} %get-tuple-element.13.own), custom_call_target="tpu_custom_call" | custom-call | tf_op jit(solution)/shard_map/share/pallas_call | solution.py:393
  71.3 57.4 %force.1 = f32[3,16,256]{2,1,0:T(8,128)} custom-call(f32[144,8,256]{2,1,0:T(8,128)} %bitcast.4, f32[9,16,256]{2,1,0:T(8,128)} %get-tuple-element.12.snd_in, f32[9,16,256]{2,1,0:T(8,128)} %share.1.rho_in, s32[9,2,128]{2,1,0:T(2,128)} %get-tuple-element.10.meta_in, s32[384]{0:T(512)} %get-tuple-element.14.tab_in, f32[376,8,128]{2,1,0:T(8,128)} %get-tuple-element.15.buf_in), custom_call_target="tpu_custom_call" | custom-call | tf_op jit(solution)/shard_map/force/pallas_call | solution.py:196

commit v3 on v2

--- a/solution.py
+++ b/solution.py
@@ -56,10 +56,28 @@
         return 0
     lax.fori_loop(0,NPAIRS,put,0,unroll=unroll)
 
-def spread(icol, f, row):
-    for half in range(2):
-        part=slice(128*half,128*half+128)
-        icol[f,part,:]=jnp.broadcast_to(row[:,part],(128,128)).T
+def split3(v):
+    high=v.astype(jnp.bfloat16)
+    rest=v-high.astype(jnp.float32)
+    middle=rest.astype(jnp.bfloat16)
+    return high,middle,(rest-middle.astype(jnp.float32)).astype(jnp.bfloat16)
+
+def pick(height, left, right):
+    k=lax.rem(lax.broadcasted_iota(jnp.int32,(3*height,256),0),height)
+    lane=lax.broadcasted_iota(jnp.int32,(3*height,256),1)
+    return (k==jnp.where(lane<128,left,right)).astype(jnp.float32).astype(jnp.bfloat16)
+
+def columns(icol, block, rows, by_matrix):
+    height=block.shape[0]
+    parts=jnp.concatenate(split3(block),0)
+    for f in range(0,by_matrix,2):
+        both=lax.dot_general(parts,pick(height,rows[f],rows[f+1]),(((0,),(0,)),((),())),preferred_element_type=jnp.float32)
+        icol[f]=both[:,0:128]
+        icol[f+1]=both[:,128:256]
+    for f in range(by_matrix,len(rows)):
+        for half in range(2):
+            lanes=slice(128*half,128*half+128)
+            icol[f,lanes,:]=jnp.broadcast_to(block[rows[f]:rows[f]+1,lanes],(128,128)).T
 
 def fetch(pairs_of_refs, sems):
     copies=[pltpu.make_async_copy(src,dst,sems.at[k]) for k,(src,dst) in enumerate(pairs_of_refs)]
@@ -67,7 +85,7 @@
         copy.start()
     return copies
 
-def density_kernel(IB,JB,U,rec_in,meta_in,pairs_in,rho,safe,tab,buf_out,rec,meta,pairs,buf,sems,filled,count_of,shifts,icol,acc):
+def density_kernel(MD,J64,J32,J16,U,rec_in,meta_in,pairs_in,rho,safe,tab,buf_out,rec,meta,pairs,buf,sems,filled,count_of,shifts,icol,acc):
     copies=fetch(((meta_in,meta),(pairs_in,pairs),(rec_in,rec)),sems)
     copies[0].wait(); copies[1].wait()
     plan(meta,pairs,tab,filled,count_of)
@@ -76,23 +94,21 @@
     leave=pltpu.make_async_copy(buf,buf_out,sems.at[3])
     leave.start()
     def cell(a,_):
-        for f,rw in enumerate((0,1,2,4)):
-            spread(icol,f,rec[a,rw:rw+1,:])
+        columns(icol,rec[a],(0,1,2,4),MD)
         first=tab[FIRST+a]; last=tab[LAST+a]
-        nfull=(last-first)//JB
         count=meta[0,0,a]
-        def iblock(g,_):
-            rows=pl.ds(pl.multiple_of(g*IB,IB),IB)
+        def iblock(IB,JB,start,_):
+            rows=pl.ds(pl.multiple_of(start,16),IB)
+            nfull=(last-first)//JB
             xi,yi,zi,hi=(icol[f,rows,:] for f in range(4))
             def tile(t):
                 j=lambda rw: buf[t,rw:rw+1,:]
                 dx=xi-j(0); dy=yi-j(1); dz=zi-j(2)
                 r2=dx*dx+dy*dy+dz*dz
                 s=hi+j(4)
-                inv=rcp(s)
-                r=r2*lax.rsqrt(jnp.maximum(r2,1e-30))
-                w=jnp.maximum(inv-r*(inv*inv),0.0)
-                t_=w*s
+                u=rcp(s*lax.rsqrt(r2))
+                t_=jnp.maximum(1.0-u,0.0)
+                w=t_*rcp(s)
                 return (w*w)*(w*t_)*((1.25-t_)*j(3))
             def many(k,total):
                 t=first+k*JB
@@ -102,7 +118,12 @@
                 total=lax.fori_loop(first+nfull*JB,last,lambda t,tt:tt+tile(t),total)
             acc[a,rows,:]=total
             return 0
-        lax.fori_loop(0,(count+IB-1)//IB,iblock,0)
+        groups=lax.shift_right_logical(count+15,4)
+        rest=lax.bitwise_and(groups,3)
+        big=lax.shift_right_logical(groups+1,2)
+        lax.fori_loop(0,big,lambda g,c:iblock(64,J64,g*64,c),0)
+        lax.fori_loop(0,jnp.where(rest==2,1,0),lambda g,c:iblock(32,J32,big*64,c),0)
+        lax.fori_loop(0,jnp.where(rest==1,1,0),lambda g,c:iblock(16,J16,big*64,c),0)
         return 0
     lax.fori_loop(0,CELLS,cell,0)
     for a in range(CELLS):
@@ -112,16 +133,16 @@
         safe[a:a+1,:]=jnp.where(there,(32.0*NORM)*sums,1.0)
     leave.wait()
 
-def density(rec,meta,pairs,IB=64,JB=2,U=8):
+def density(rec,meta,pairs,J64=2,J32=4,J16=4,U=8,M_=None):
     V=pl.BlockSpec(memory_space=pltpu.VMEM); S=pl.BlockSpec(memory_space=pltpu.SMEM); H=pl.BlockSpec(memory_space=pltpu.HBM)
-    return pl.pallas_call(functools.partial(density_kernel,IB,JB,U),
+    return pl.pallas_call(functools.partial(density_kernel,0 if M_ is None else M_,J64,J32,J16,U),
         out_shape=(jax.ShapeDtypeStruct((CELLS,SLOTS),jnp.float32),jax.ShapeDtypeStruct((CELLS,SLOTS),jnp.float32),jax.ShapeDtypeStruct((384,),jnp.int32),jax.ShapeDtypeStruct((MAXT,8,128),jnp.float32)),
         in_specs=[H,H,H],out_specs=(V,V,S,H),
         scratch_shapes=[pltpu.VMEM((144,8,SLOTS),jnp.float32),pltpu.SMEM((9,2,128),jnp.int32),pltpu.SMEM((3,NPAIRS),jnp.int32),pltpu.VMEM((MAXT,8,128),jnp.float32),pltpu.SemaphoreType.DMA((4,)),pltpu.SMEM((CELLS,),jnp.int32),pltpu.SMEM((NPAIRS,),jnp.int32),pltpu.VMEM((27,8,128),jnp.float32),pltpu.VMEM((4,SLOTS,128),jnp.float32),pltpu.VMEM((CELLS,SLOTS,128),jnp.float32)],
         compiler_params=pltpu.CompilerParams(vmem_limit_bytes=WHOLE),
         name="density")(rec,meta,pairs)
 
-def force_kernel(IB,JB,U,rec_in,snd_in,rho_in,meta_in,tab_in,buf_in,out,rec,snd,rho,meta,tab,buf,sems,extra,cells,icol,acc):
+def force_kernel(MF,J32,J16,U,rec_in,snd_in,rho_in,meta_in,tab_in,buf_in,out,rec,snd,rho,meta,tab,buf,sems,extra,cells,icol,acc):
     copies=fetch(((snd_in,snd),(rho_in,rho),(tab_in,tab),(meta_in.at[0],meta.at[0]),(rec_in.at[pl.ds(0,CELLS)],rec),(buf_in,buf)),sems)
     for copy in copies[:4]:
         copy.wait()
@@ -143,16 +164,15 @@
     for copy in copies[4:]:
         copy.wait()
     def cell(a,_):
-        for f,rw in enumerate((0,1,2,4,5,6,7)):
-            spread(icol,f,rec[a,rw:rw+1,:])
-        for f in range(3):
-            for half in range(2):
-                icol[7+f,128*half:128*half+128,:]=jnp.broadcast_to(cells[half,pl.ds(a*8+f,1),:],(128,128)).T
+        own=pl.ds(pl.multiple_of(a*8,8),8)
+        more=jnp.concatenate([cells[0,own,:],cells[1,own,:]],1)
+        more=jnp.where(lax.broadcasted_iota(jnp.int32,(8,SLOTS),0)<3,more,0.0)
+        columns(icol,jnp.concatenate([rec[a],more],0),(0,1,2,4,5,6,7,8,9,10),MF)
         first=tab[FIRST+a]; last=tab[LAST+a]
-        nfull=(last-first)//JB
         count=meta[0,0,a]
-        def iblock(g,_):
-            rows=pl.ds(pl.multiple_of(g*IB,IB),IB)
+        def iblock(IB,JB,start,_):
+            rows=pl.ds(pl.multiple_of(start,16),IB)
+            nfull=(last-first)//JB
             def tile(t):
                 i=lambda f: icol[f,rows,:]
                 j=lambda rw: buf[t,rw:rw+1,:]
@@ -161,13 +181,12 @@
                 r2=dx*dx+dy*dy+dz*dz
                 s=i(3)+j(4)
                 inv=rcp(s)
-                r=r2*lax.rsqrt(jnp.maximum(r2,1e-30))
-                i2=inv*inv
-                w=jnp.maximum(inv-r*i2,0.0)
+                u=rcp(s*lax.rsqrt(r2))
+                w=jnp.maximum(1.0-u,0.0)*inv
                 va=jnp.minimum((i(4)-j(5))*dx+(i(5)-j(6))*dy+(i(6)-j(7))*dz,0.0)
-                m=s*va*rcp(r2+0.0025*(s*s))
+                m=va*inv*rcp(u*u+0.0025)
                 visc=m*((m-i(7))-e(0))*rcp(i(9)+e(2))
-                f=(i(8)+e(1)+visc)*j(3)*((w*w)*(w*i2))
+                f=(i(8)+e(1)+visc)*j(3)*((w*w)*(w*(inv*inv)))
                 return f*dx,f*dy,f*dz
             def many(k,total):
                 t=first+k*JB
@@ -183,7 +202,10 @@
             for c in range(3):
                 acc[c,a,rows,:]=total[c]
             return 0
-        lax.fori_loop(0,(count+IB-1)//IB,iblock,0)
+        groups=lax.shift_right_logical(count+15,4)
+        big=lax.shift_right_logical(groups,1)
+        lax.fori_loop(0,big,lambda g,c:iblock(32,J32,g*32,c),0)
+        lax.fori_loop(0,lax.bitwise_and(groups,1),lambda g,c:iblock(16,J16,big*32,c),0)
         return 0
     lax.fori_loop(0,CELLS,cell,0)
     for a in range(CELLS):
@@ -191,9 +213,9 @@
             sums=jnp.sum(acc[c,a].T,axis=0,keepdims=True)
             out[c,a:a+1,:]=jnp.where(rec[a,3:4,:]>0,(160.0*NORM)*sums,0.0)
 
-def force(rec,snd,rho,meta,tab,buf,IB=32,JB=2,U=8):
+def force(rec,snd,rho,meta,tab,buf,J32=4,J16=4,U=8,M_=None):
     V=pl.BlockSpec(memory_space=pltpu.VMEM); S=pl.BlockSpec(memory_space=pltpu.SMEM); H=pl.BlockSpec(memory_space=pltpu.HBM)
-    return pl.pallas_call(functools.partial(force_kernel,IB,JB,U),
+    return pl.pallas_call(functools.partial(force_kernel,6 if M_ is None else M_,J32,J16,U),
         out_shape=jax.ShapeDtypeStruct((3,CELLS,SLOTS),jnp.float32),
         in_specs=[H]*6,out_specs=V,
         scratch_shapes=[pltpu.VMEM((CELLS,8,SLOTS),jnp.float32),pltpu.VMEM((9,CELLS,SLOTS),jnp.float32),pltpu.VMEM((9,CELLS,SLOTS),jnp.float32),pltpu.SMEM((1,2,128),jnp.int32),pltpu.SMEM((384,),jnp.int32),pltpu.VMEM((MAXT,8,128),jnp.float32),pltpu.SemaphoreType.DMA((6,)),pltpu.VMEM((MAXT,8,128),jnp.float32),pltpu.VMEM((2,144*8,128),jnp.float32),pltpu.VMEM((10,SLOTS,128),jnp.float32),pltpu.VMEM((3,CELLS,SLOTS,128),jnp.float32)],
@@ -206,6 +228,7 @@
 N_GX=16; N_GY=8
 AROUND=((-1,-1),(-1,0),(-1,1),(0,-1),(0,1),(1,-1),(1,0),(1,1))
 MESH=pl.DeviceIdType.MESH
+ITEMS=(0, 1, 2, 3)
 
 
 def neighbours(u, w):
@@ -224,9 +247,8 @@
     barrier = pltpu.get_barrier_semaphore()
     for off in range(1, N_GX):
         pl.semaphore_signal(barrier, inc=1, device_id=(lax.rem(u + off, N_GX), w), device_id_type=MESH)
-    for n, (du, dw) in enumerate(AROUND):
-        if dw != 0:
-            pl.semaphore_signal(barrier, inc=1, device_id=around[n], device_id_type=MESH)
+    for n in (3, 4):
+        pl.semaphore_signal(barrier, inc=1, device_id=around[n], device_id_type=MESH)
 
     for copy in loads:
         copy.wait()
@@ -264,7 +286,7 @@
         return 0
 
     lax.fori_loop(0, N_GX, post, 0)
-    pl.semaphore_wait(barrier, N_GX - 1 + 6)
+    pl.semaphore_wait(barrier, N_GX - 1 + 2)
 
     def parcel(off):
         return pltpu.make_async_remote_copy(
@@ -310,19 +332,36 @@
     metas[0:1, :] = amounts.astype(jnp.int32)
     metas[1:2, :] = lists[...]
 
-    copies = []
-    own = ((metas, meta_out), (moved, rec_out), (sounds_moved, snd_out))
-    for n in range(8):
-        for k, (src, dst) in enumerate(own):
-            copy = pltpu.make_async_remote_copy(
-                src_ref=src, dst_ref=dst.at[n + 1], send_sem=send2.at[n, k], recv_sem=recv2.at[n, k],
-                device_id=around[n], device_id_type=MESH)
+    halves = (pl.ds(0, 8), pl.ds(8, 8))
+    own = (metas, moved.at[halves[0]], moved.at[halves[1]], sounds_moved)
+    at = lambda n: (meta_out.at[n], rec_out.at[n, halves[0]], rec_out.at[n, halves[1]], snd_out.at[n])
+    remote = lambda src, n, k, device: pltpu.make_async_remote_copy(
+        src_ref=src, dst_ref=at(n + 1)[k], send_sem=send2.at[n, k], recv_sem=recv2.at[n, k],
+        device_id=device, device_id_type=MESH)
+    copies, arriving = [], {}
+    for k in ITEMS:
+        for n in (1, 6):
+            copy = remote(own[k], n, k, around[n])
+            copy.start()
+            arriving[n, k] = copy
+    for k in ITEMS:
+        for n in (3, 4):
+            copy = remote(own[k], n, k, around[n])
             copy.start()
             copies.append(copy)
-    for k, (src, dst) in enumerate(own):
-        copy = pltpu.make_async_copy(src, dst.at[0], load.at[k])
+    for k in range(4):
+        copy = pltpu.make_async_copy(own[k], at(0)[k], load.at[k])
         copy.start()
         copies.append(copy)
+    for k in ITEMS:
+        for n in (1, 6):
+            arriving[n, k].wait_recv()
+            for to, step in ((n - 1, 3), (n + 1, 4)):
+                copy = remote(at(n + 1)[k], to, k, around[step])
+                copy.start()
+                copies.append(copy)
+    for copy in arriving.values():
+        copy.wait_send()
 
     def sent(off, _):
         parcel(off).wait_send()
@@ -362,8 +401,8 @@
             pltpu.SemaphoreType.DMA((8,)),
             pltpu.SemaphoreType.DMA((N_GX,)),
             pltpu.SemaphoreType.DMA((N_GX,)),
-            pltpu.SemaphoreType.DMA((8, 3)),
-            pltpu.SemaphoreType.DMA((8, 3)),
+            pltpu.SemaphoreType.DMA((8, 4)),
+            pltpu.SemaphoreType.DMA((8, 4)),
         ],
         compiler_params=pltpu.CompilerParams(collective_id=0, has_side_effects=True, vmem_limit_bytes=WHOLE),
         name="exchange",

time: 129 us -> 116 us (0.90)
  the two profiles are of different devices: /device:TPU:25 before, /device:TPU:13 now
where the time goes in v3:
time: 116 us
  Pallas kernels  115 us (99%)
    pallas_call x1, Pallas kernels, force(): pl.pallas_call(functools.partial(force_kernel, 6 if M_ is None else M_, J...  54.7 us
    pallas_call x1, Pallas kernels, density(): pl.pallas_call(functools.partial(density_kernel, 0 if M_ is None else M_,...  29.6 us
    pallas_call x1, Pallas kernels, exchange(): pl.pallas_call(exchange_kernel, out_shape=(jax.ShapeDtypeStruct((9, 16, 8...  23.8 us
    pallas_call x1, Pallas kernels, share(): pl.pallas_call(share_kernel, out_shape=jax.ShapeDtypeStruct((9, 16, 256),...  6.89 us

profile of v3, /device:TPU:13, one launch (start us, length us, event | category | flops | bytes accessed | tf_op | source)
XLA Modules:
  0.0 115.6 jit_solution(12691800294383390090)
XLA Ops:
  0.6 23.8 %exchange.1 = (f32[9,16,8,256]{3,2,1,0:T(8,128)}, f32[9,16,256]{2,1,0:T(8,128)}, s32[9,2,128]{2,1,0:T(2,128)}) custom-call(f32[3,16,256]{2,1,0:T(8,128)} %refs_0_.1, f32[3,16,256]{2,1,0:T(8,128)} %refs_1_.1, f32[16,256]{1,0:T(8,128)} %refs_2_.1, f32[16,256]{1,0:T(8,128)} %refs_3_.1, f32[16,256]{1,0:T(8,128)} %refs_4_.1, s32[16]{0:T(128)} %refs_5_.1, ...), custom_call_target="tpu_custom_call" | custom-call | tf_op jit(solution)/shard_map/exchange/pallas_call | solution.py:379
  24.4 29.6 %density.1 = (f32[16,256]{1,0:T(8,128)}, f32[16,256]{1,0:T(8,128)}, s32[384]{0:T(512)}, f32[376,8,128]{2,1,0:T(8,128)}) custom-call(f32[144,8,256]{2,1,0:T(8,128)} %bitcast.3, s32[9,2,128]{2,1,0:T(2,128)} %get-tuple-element.10.meta_in, s32[3,160]{1,0:T(4,128)} %bitcast.5), custom_call_target="tpu_custom_call" | custom-call | tf_op jit(solution)/shard_map/density/pallas_call | solution.py:138
  54.0 6.9 %share.1.rho_in = f32[9,16,256]{2,1,0:T(8,128)} custom-call(f32[16,256]{1,0:T(8,128)} %get-tuple-element.13.own), custom_call_target="tpu_custom_call" | custom-call | tf_op jit(solution)/shard_map/share/pallas_call | solution.py:432
  60.9 54.7 %force.1 = f32[3,16,256]{2,1,0:T(8,128)} custom-call(f32[144,8,256]{2,1,0:T(8,128)} %bitcast.4, f32[9,16,256]{2,1,0:T(8,128)} %get-tuple-element.12.snd_in, f32[9,16,256]{2,1,0:T(8,128)} %share.1.rho_in, s32[9,2,128]{2,1,0:T(2,128)} %get-tuple-element.10.meta_in, s32[384]{0:T(512)} %get-tuple-element.14.tab_in, f32[376,8,128]{2,1,0:T(8,128)} %get-tuple-element.15.buf_in), custom_call_target="tpu_custom_call" | custom-call | tf_op jit(solution)/shard_map/force/pallas_call | solution.py:218

commit v4 on v3

v4 whole, which is shorter than its diff:
```python
import math, functools
import jax, jax.numpy as jnp
from jax import lax
from jax.experimental import pallas as pl
from jax.experimental.pallas import tpu as pltpu

CELLS=16; SLOTS=256; NPAIRS=160; NORM=21.0/(16.0*math.pi)
WHOLE=63<<20
MAXT=2*NPAIRS+3*CELLS+8
PLACE=NPAIRS; FIRST=2*NPAIRS; LAST=FIRST+CELLS

def rcp(x):
    return pl.reciprocal(x, approx=True)

def append(buf, x0, x1, pos, lane):
    tile=lax.shift_right_logical(pos,7); s=lax.bitwise_and(pos,127)
    t0=pltpu.roll(x0,s,1); t1=pltpu.roll(x1,s,1)
    keep=lane>=s
    pltpu.store(buf.at[tile],t0,mask=keep)
    buf[tile+1]=jnp.where(keep,t1,t0)
    buf[tile+2]=jnp.where(keep,0.0,t1)

def plan(meta, pairs, tab, filled, count_of, place_of):
    for a in range(CELLS):
        filled[a]=0
    def size(p,_):
        a=pairs[0,p]; b=pairs[1,p]
        n=lax.shift_right_logical(b,4); r=lax.bitwise_and(b,15)
        cell=jnp.where(n==0,r,meta[n,1,jnp.maximum(n-1,0)*16+r])
        count=meta[n,0,cell]
        tab[p]=n*16+cell
        place_of[p]=n*16+meta[n,2,cell]
        count_of[p]=count
        filled[a]=filled[a]+count
        return 0
    lax.fori_loop(0,NPAIRS,size,0,unroll=8)
    tile=jnp.int32(0)
    for a in range(CELLS):
        end=tile+lax.shift_right_logical(filled[a]+127,7)
        tab[FIRST+a]=tile; tab[LAST+a]=end
        filled[a]=tile*128
        tile=end+2

def pack_main(rec, pairs, tab, filled, count_of, place_of, shifts, buf, unroll):
    lane=lax.broadcasted_iota(jnp.int32,(8,128),1)
    row=lax.broadcasted_iota(jnp.int32,(8,128),0)
    for d in range(27):
        dx,dy,dz=d//9-1,d//3%3-1,d%3-1
        shifts[d]=jnp.where(row==0,float(dx),jnp.where(row==1,float(dy),jnp.where(row==2,float(dz),0.0)))
    def put(p,_):
        a=pairs[0,p]
        pos=filled[a]
        filled[a]=pos+count_of[p]
        tab[PLACE+p]=pos
        src=place_of[p]; shift=shifts[pairs[2,p]]
        append(buf,rec[src,:,0:128]+shift,rec[src,:,128:256]+shift,pos,lane)
        return 0
    lax.fori_loop(0,NPAIRS,put,0,unroll=unroll)

def columns(icol, block, rows):
    for f,row in enumerate(rows):
        for half in range(2):
            lanes=slice(128*half,128*half+128)
            icol[f,lanes,:]=jnp.broadcast_to(block[row:row+1,lanes],(128,128)).T

def extra_fields(c2, rho):
    return 0.5*(c2*lax.rsqrt(c2)),c2*rcp(rho),rho

def fetch(pairs_of_refs, sems):
    copies=[pltpu.make_async_copy(src,dst,sems.at[k]) for k,(src,dst) in enumerate(pairs_of_refs)]
    for copy in copies:
        copy.start()
    return copies

def density_kernel(J64,J32,J16,U,rec_in,meta_in,pairs_in,cols_in,rho,safe,tab,buf_out,rec,meta,pairs,buf,sems,filled,count_of,place_of,shifts,cols,col_sems,acc):
    copies=fetch(((meta_in,meta),(pairs_in,pairs),(rec_in,rec)),sems)
    copies[0].wait(); copies[1].wait()
    def column_copy(a):
        return pltpu.make_async_copy(cols_in.at[meta[0,2,a],pl.ds(0,4)],cols.at[a],col_sems.at[a])
    def ask(a,_):
        column_copy(a).start()
        return 0
    lax.fori_loop(0,CELLS,ask,0)
    plan(meta,pairs,tab,filled,count_of,place_of)
    copies[2].wait()
    pack_main(rec,pairs,tab,filled,count_of,place_of,shifts,buf,U)
    leave=pltpu.make_async_copy(buf,buf_out,sems.at[3])
    leave.start()
    def cell(a,_):
        column_copy(a).wait()
        icol=cols.at[a]
        first=tab[FIRST+a]; last=tab[LAST+a]
        count=meta[0,0,a]
        def iblock(IB,JB,start,_):
            rows=pl.ds(pl.multiple_of(start,16),IB)
            nfull=(last-first)//JB
            xi,yi,zi,hi=(icol[f,rows,:] for f in range(4))
            def tile(t):
                j=lambda rw: buf[t,rw:rw+1,:]
                dx=xi-j(0); dy=yi-j(1); dz=zi-j(2)
                r2=dx*dx+dy*dy+dz*dz
                s=hi+j(4)
                u=rcp(s*lax.rsqrt(r2))
                t_=jnp.maximum(1.0-u,0.0)
                w=t_*rcp(s)
                return (w*w)*(w*t_)*((1.25-t_)*j(3))
            def many(k,total):
                t=first+k*JB
                return total+functools.reduce(lambda p,q:p+q,[tile(t+i) for i in range(JB)])
            total=lax.fori_loop(0,nfull,many,jnp.zeros((IB,128),jnp.float32))
            if JB>1:
                total=lax.fori_loop(first+nfull*JB,last,lambda t,tt:tt+tile(t),total)
            acc[a,rows,:]=total
            return 0
        groups=lax.shift_right_logical(count+15,4)
        rest=lax.bitwise_and(groups,3)
        big=lax.shift_right_logical(groups+1,2)
        lax.fori_loop(0,big,lambda g,c:iblock(64,J64,g*64,c),0)
        lax.fori_loop(0,jnp.where(rest==2,1,0),lambda g,c:iblock(32,J32,big*64,c),0)
        lax.fori_loop(0,jnp.where(rest==1,1,0),lambda g,c:iblock(16,J16,big*64,c),0)
        return 0
    lax.fori_loop(0,CELLS,cell,0)
    for a in range(CELLS):
        sums=jnp.sum(acc[a].T,axis=0,keepdims=True)
        there=rec[meta[0,2,a],3:4,:]>0
        rho[a:a+1,:]=jnp.where(there,(32.0*NORM)*sums,0.0)
        safe[a:a+1,:]=jnp.where(there,(32.0*NORM)*sums,1.0)
    leave.wait()

def density(rec,meta,pairs,cols,J64=2,J32=4,J16=4,U=8):
    V=pl.BlockSpec(memory_space=pltpu.VMEM); S=pl.BlockSpec(memory_space=pltpu.SMEM); H=pl.BlockSpec(memory_space=pltpu.HBM)
    return pl.pallas_call(functools.partial(density_kernel,J64,J32,J16,U),
        out_shape=(jax.ShapeDtypeStruct((CELLS,SLOTS),jnp.float32),jax.ShapeDtypeStruct((CELLS,SLOTS),jnp.float32),jax.ShapeDtypeStruct((384,),jnp.int32),jax.ShapeDtypeStruct((MAXT,8,128),jnp.float32)),
        in_specs=[H,H,H,H],out_specs=(V,V,S,H),
        scratch_shapes=[pltpu.VMEM((144,8,SLOTS),jnp.float32),pltpu.SMEM((9,4,128),jnp.int32),pltpu.SMEM((3,NPAIRS),jnp.int32),pltpu.VMEM((MAXT,8,128),jnp.float32),pltpu.SemaphoreType.DMA((4,)),pltpu.SMEM((CELLS,),jnp.int32),pltpu.SMEM((NPAIRS,),jnp.int32),pltpu.SMEM((NPAIRS,),jnp.int32),pltpu.VMEM((27,8,128),jnp.float32),pltpu.VMEM((CELLS,4,SLOTS,128),jnp.float32),pltpu.SemaphoreType.DMA((CELLS,)),pltpu.VMEM((CELLS,SLOTS,128),jnp.float32)],
        compiler_params=pltpu.CompilerParams(vmem_limit_bytes=WHOLE),
        name="density")(rec,meta,pairs,cols)

def force_kernel(J32,J16,U,rec_in,snd_in,rho_in,meta_in,tab_in,buf_in,cols_in,rest_in,out,rec,snd,rho,meta,tab,buf,sems,extra,cells,cols,col_sems,acc):
    copies=fetch(((snd_in,snd),(rho_in,rho),(tab_in,tab),(meta_in.at[0],meta.at[0]),(rec_in.at[pl.ds(0,CELLS)],rec),(buf_in,buf)),sems)
    copies[3].wait()
    def column_copy(a):
        return (pltpu.make_async_copy(cols_in.at[meta[0,2,a]],cols.at[a,pl.ds(0,7)],col_sems.at[0,a]),
                pltpu.make_async_copy(rest_in.at[a],cols.at[a,pl.ds(7,3)],col_sems.at[1,a]))
    def ask(a,_):
        for copy in column_copy(a):
            copy.start()
        return 0
    lax.fori_loop(0,CELLS,ask,0)
    for copy in copies[:3]:
        copy.wait()
    for n in range(9):
        for half in range(2):
            c8=slice(8*half,8*half+8)
            c2=snd[n,c8,:]; rr=rho[n,c8,:]
            base=(n*16+8*half)*8
            for f,val in enumerate(extra_fields(c2,rr)):
                cells[0,pl.ds(base+f,8,stride=8),:]=val[:,0:128]
                cells[1,pl.ds(base+f,8,stride=8),:]=val[:,128:256]
    lane=lax.broadcasted_iota(jnp.int32,(8,128),1)
    block=lambda src: pl.ds(pl.multiple_of(src*8,8),8)
    def put(p,_):
        src=tab[p]
        append(extra,cells[0,block(src),:],cells[1,block(src),:],tab[PLACE+p],lane)
        return 0
    lax.fori_loop(0,NPAIRS,put,0,unroll=U)
    for copy in copies[4:]:
        copy.wait()
    def cell(a,_):
        for copy in column_copy(a):
            copy.wait()
        first=tab[FIRST+a]; last=tab[LAST+a]
        count=meta[0,0,a]
        def iblock(IB,JB,start,_):
            rows=pl.ds(pl.multiple_of(start,16),IB)
            nfull=(last-first)//JB
            def tile(t):
                i=lambda f: cols[a,f,rows,:]
                j=lambda rw: buf[t,rw:rw+1,:]
                e=lambda rw: extra[t,rw:rw+1,:]
                dx=i(0)-j(0); dy=i(1)-j(1); dz=i(2)-j(2)
                r2=dx*dx+dy*dy+dz*dz
                s=i(3)+j(4)
                inv=rcp(s)
                u=rcp(s*lax.rsqrt(r2))
                w=jnp.maximum(1.0-u,0.0)*inv
                va=jnp.minimum((i(4)-j(5))*dx+(i(5)-j(6))*dy+(i(6)-j(7))*dz,0.0)
                m=va*inv*rcp(u*u+0.0025)
                visc=m*((m-i(7))-e(0))*rcp(i(9)+e(2))
                f=(i(8)+e(1)+visc)*j(3)*((w*w)*(w*(inv*inv)))
                return f*dx,f*dy,f*dz
            def many(k,total):
                t=first+k*JB
                ts=[tile(t+q) for q in range(JB)]
                return tuple(total[c]+functools.reduce(lambda p,q:p+q,[x[c] for x in ts]) for c in range(3))
            z=jnp.zeros((IB,128),jnp.float32)
            total=lax.fori_loop(0,nfull,many,(z,z,z))
            if JB>1:
                def one(t,tt):
                    x=tile(t)
                    return tuple(p+q for p,q in zip(tt,x))
                total=lax.fori_loop(first+nfull*JB,last,one,total)
            for c in range(3):
                acc[c,a,rows,:]=total[c]
            return 0
        groups=lax.shift_right_logical(count+15,4)
        big=lax.shift_right_logical(groups,1)
        lax.fori_loop(0,big,lambda g,c:iblock(32,J32,g*32,c),0)
        lax.fori_loop(0,lax.bitwise_and(groups,1),lambda g,c:iblock(16,J16,big*32,c),0)
        return 0
    lax.fori_loop(0,CELLS,cell,0)
    for a in range(CELLS):
        for c in range(3):
            sums=jnp.sum(acc[c,a].T,axis=0,keepdims=True)
            out[c,a:a+1,:]=jnp.where(rec[meta[0,2,a],3:4,:]>0,(160.0*NORM)*sums,0.0)

def force(rec,snd,rho,meta,tab,buf,cols,rest,J32=4,J16=4,U=8):
    V=pl.BlockSpec(memory_space=pltpu.VMEM); S=pl.BlockSpec(memory_space=pltpu.SMEM); H=pl.BlockSpec(memory_space=pltpu.HBM)
    return pl.pallas_call(functools.partial(force_kernel,J32,J16,U),
        out_shape=jax.ShapeDtypeStruct((3,CELLS,SLOTS),jnp.float32),
        in_specs=[H]*8,out_specs=V,
        scratch_shapes=[pltpu.VMEM((CELLS,8,SLOTS),jnp.float32),pltpu.VMEM((9,CELLS,SLOTS),jnp.float32),pltpu.VMEM((9,CELLS,SLOTS),jnp.float32),pltpu.SMEM((1,4,128),jnp.int32),pltpu.SMEM((384,),jnp.int32),pltpu.VMEM((MAXT,8,128),jnp.float32),pltpu.SemaphoreType.DMA((6,)),pltpu.VMEM((MAXT,8,128),jnp.float32),pltpu.VMEM((2,144*8,128),jnp.float32),pltpu.VMEM((CELLS,10,SLOTS,128),jnp.float32),pltpu.SemaphoreType.DMA((2,CELLS)),pltpu.VMEM((3,CELLS,SLOTS,128),jnp.float32)],
        compiler_params=pltpu.CompilerParams(vmem_limit_bytes=WHOLE),
        name="force")(rec,snd,rho,meta,tab,buf,cols,rest)


from jax.sharding import PartitionSpec as P

N_GX=16; N_GY=8
AROUND=((-1,-1),(-1,0),(-1,1),(0,-1),(0,1),(1,-1),(1,0),(1,1))
MESH=pl.DeviceIdType.MESH
OWN_FIELDS=(0, 1, 2, 4, 5, 6, 7)


def neighbours(u, w):
    return [(lax.rem(u + du + N_GX, N_GX), lax.rem(w + dw + N_GY, N_GY)) for du, dw in AROUND]


def exchange_kernel(*refs):
    given, (rec_out, snd_out, meta_out, cols_out), scratch = refs[:8], refs[8:12], refs[12:]
    held, (rec, outbox, inbox, outbox2, inbox2, metas, moved, sounds_moved, cols, load, leave, send1, recv1, send2, recv2) = scratch[:8], scratch[8:]
    pos, vel, mass, smooth, snd, counts, move, lists = held
    u, w = lax.axis_index("gx"), lax.axis_index("gy")
    loads = [pltpu.make_async_copy(src, dst, load.at[k]) for k, (src, dst) in enumerate(zip(given, held))]
    for copy in loads:
        copy.start()
    around = neighbours(u, w)
    barrier = pltpu.get_barrier_semaphore()
    for off in range(1, N_GX):
        pl.semaphore_signal(barrier, inc=1, device_id=(lax.rem(u + off, N_GX), w), device_id_type=MESH)
    for n in (3, 4):
        pl.semaphore_signal(barrier, inc=1, device_id=around[n], device_id_type=MESH)

    for copy in loads:
        copy.wait()
    slot = lax.broadcasted_iota(jnp.int32, (1, 256), 1)
    for c in range(16):
        for f in range(3):
            rec[c, f:f + 1, :] = pos[f, c:c + 1, :]
            rec[c, 5 + f:6 + f, :] = vel[f, c:c + 1, :]
        rec[c, 3:4, :] = jnp.where(slot < counts[c], mass[c:c + 1, :], 0.0)
        rec[c, 4:5, :] = smooth[c:c + 1, :]

    headed = [lax.shift_right_logical(move[c], 7) for c in range(16)]
    row = lax.broadcasted_iota(jnp.int32, (8, 256), 0)

    def post(off, _):
        column = lax.rem(u + off, N_GX)
        first, last = jnp.int32(16), jnp.int32(-1)
        for c in range(16):
            match = headed[c] == column
            first = jnp.minimum(first, jnp.where(match, c, 16))
            last = jnp.where(match, c, last)
        found = last >= 0
        first = jnp.where(found, first, 0)
        last = jnp.where(found, last, 0)
        outbox[off, 0:8, :] = rec[first]
        outbox2[off] = rec[last]
        number = lambda c: jnp.where(found, move[c], -1).astype(jnp.float32)
        amount = lambda c: counts[c].astype(jnp.float32)
        more = jnp.where(row == 0, snd[pl.ds(first, 1), :], snd[pl.ds(last, 1), :])
        more = jnp.where(row == 2, number(first), more)
        more = jnp.where(row == 3, number(last), more)
        more = jnp.where(row == 4, amount(first), more)
        more = jnp.where(row == 5, amount(last), more)
        outbox[off, 8:16, :] = more
        return 0

    lax.fori_loop(0, N_GX, post, 0)
    pl.semaphore_wait(barrier, N_GX - 1 + 2)

    def parcel(off, part):
        src, dst = ((outbox, inbox), (outbox2, inbox2))[part]
        return pltpu.make_async_remote_copy(
            src_ref=src.at[off], dst_ref=dst.at[off], send_sem=send1.at[part, off], recv_sem=recv1.at[part, off],
            device_id=(lax.rem(u + off, N_GX), w), device_id_type=MESH)

    for part in range(2):
        def start(off, _):
            parcel(off, part).start()
            return 0

        lax.fori_loop(1, N_GX, start, 0)
    inbox[0] = outbox[0]
    inbox2[0] = outbox2[0]

    first_own = ((u * N_GY + w) * 16).astype(jnp.float32)
    sub = lax.broadcasted_iota(jnp.int32, (16, 256), 0).astype(jnp.float32) + first_own
    lane = lax.broadcasted_iota(jnp.int32, (1, 128), 1).astype(jnp.float32) + first_own

    def place(cells, block, number, rank):
        key = jnp.broadcast_to(jnp.where(number >= 0.0, rank, -1.0), (8, 256))
        cells = tuple(jnp.where(key == float(k), block, cells[k]) for k in range(8))
        return cells, rank + jnp.where(number >= 0.0, 1.0, 0.0)

    def absorb(off, carry):
        cells, rank, sounds, amounts, ranks = carry
        for k in range(2):
            number = inbox[off, 10 + k:11 + k, :]
            mine = lane == number[:, 0:128]
            sounds = jnp.where(sub == number, inbox[off, 8 + k:9 + k, :], sounds)
            amounts = jnp.where(mine, inbox[off, 12 + k:13 + k, 0:128], amounts)
            ranks = jnp.where(mine, rank[:, 0:128] + 8.0 * k, ranks)
        cells, rank = place(cells, inbox[off, 0:8, :], inbox[off, 10:11, :], rank)
        return cells, rank, sounds, amounts, ranks

    def absorb_next(off, carry):
        parcel(off, 0).wait_recv()
        return absorb(off, carry)

    def absorb2(off, carry):
        return place(carry[0], inbox2[off], inbox[off, 10:11, :], carry[1])

    def absorb2_next(off, carry):
        parcel(off, 1).wait_recv()
        return absorb2(off, carry)

    zero = jnp.zeros((8, 256), jnp.float32)
    line = jnp.zeros((1, 128), jnp.float32)
    none = ((zero,) * 8, jnp.zeros((1, 256), jnp.float32))
    carry = absorb(0, none + (jnp.zeros((16, 256), jnp.float32), line, line))
    cells, _, sounds, amounts, ranks = lax.fori_loop(1, N_GX, absorb_next, carry)
    for k in range(8):
        moved[k] = cells[k]
    sounds_moved[...] = sounds
    metas[0:1, :] = amounts.astype(jnp.int32)
    metas[1:2, :] = lists[...]
    metas[2:3, :] = ranks.astype(jnp.int32)
    metas[3:4, :] = lists[...]

    halves = (pl.ds(0, 8), pl.ds(8, 8))
    own = (metas, moved.at[halves[0]], sounds_moved, moved.at[halves[1]])
    at = lambda n: (meta_out.at[n], rec_out.at[n, halves[0]], snd_out.at[n], rec_out.at[n, halves[1]])
    remote = lambda src, n, k, device: pltpu.make_async_remote_copy(
        src_ref=src, dst_ref=at(n + 1)[k], send_sem=send2.at[n, k], recv_sem=recv2.at[n, k],
        device_id=device, device_id_type=MESH)
    copies, arriving = [], {}

    def spread_out(items):
        for nearest in ((1, 6), (3, 4)):
            for k in items:
                for n in nearest:
                    copy = remote(own[k], n, k, around[n])
                    copy.start()
                    if nearest == (1, 6):
                        arriving[n, k] = copy
                    else:
                        copies.append(copy)

    def pass_on(items):
        for k in items:
            for n in (1, 6):
                arriving[n, k].wait_recv()
                for to, step in ((n - 1, 3), (n + 1, 4)):
                    copy = remote(at(n + 1)[k], to, k, around[step])
                    copy.start()
                    copies.append(copy)

    def column_copy(k):
        return pltpu.make_async_copy(cols.at[k], cols_out.at[k], leave.at[k])

    def make_columns(k, _):
        columns(cols.at[k], moved[k], OWN_FIELDS)
        column_copy(k).start()
        return 0

    spread_out((0, 1, 2))
    cells, _ = lax.fori_loop(1, N_GX, absorb2_next, absorb2(0, none))
    for k in range(8):
        moved[8 + k] = cells[k]
    spread_out((3,))
    for k in range(4):
        copy = pltpu.make_async_copy(own[k], at(0)[k], load.at[k])
        copy.start()
        copies.append(copy)
    pass_on((0, 1, 2, 3))
    lax.fori_loop(0, 16, make_columns, 0)
    for copy in arriving.values():
        copy.wait_send()

    def left(k, _):
        column_copy(k).wait()
        return 0

    lax.fori_loop(0, 16, left, 0)

    def sent(off, _):
        parcel(off, 0).wait_send()
        parcel(off, 1).wait_send()
        return 0

    lax.fori_loop(1, N_GX, sent, 0)
    for copy in copies:
        copy.wait()


VMEM=pl.BlockSpec(memory_space=pltpu.VMEM)
HBM=pl.BlockSpec(memory_space=pltpu.HBM)

def exchange(positions, velocities, masses, smoothing, sound2, counts, move_to, lists):
    return pl.pallas_call(
        exchange_kernel,
        out_shape=(jax.ShapeDtypeStruct((9, 16, 8, 256), jnp.float32),
                   jax.ShapeDtypeStruct((9, 16, 256), jnp.float32),
                   jax.ShapeDtypeStruct((9, 4, 128), jnp.int32),
                   jax.ShapeDtypeStruct((16, 7, 256, 128), jnp.float32)),
        in_specs=[HBM] * 8,
        out_specs=(HBM,) * 4,
        scratch_shapes=[
            pltpu.VMEM((3, 16, 256), jnp.float32),
            pltpu.VMEM((3, 16, 256), jnp.float32),
            pltpu.VMEM((16, 256), jnp.float32),
            pltpu.VMEM((16, 256), jnp.float32),
            pltpu.VMEM((16, 256), jnp.float32),
            pltpu.SMEM((16,), jnp.int32),
            pltpu.SMEM((16,), jnp.int32),
            pltpu.VMEM((1, 128), jnp.int32),
            pltpu.VMEM((16, 8, 256), jnp.float32),
            pltpu.VMEM((N_GX, 16, 256), jnp.float32),
            pltpu.VMEM((N_GX, 16, 256), jnp.float32),
            pltpu.VMEM((N_GX, 8, 256), jnp.float32),
            pltpu.VMEM((N_GX, 8, 256), jnp.float32),
            pltpu.VMEM((4, 128), jnp.int32),
            pltpu.VMEM((16, 8, 256), jnp.float32),
            pltpu.VMEM((16, 256), jnp.float32),
            pltpu.VMEM((16, 7, 256, 128), jnp.float32),
            pltpu.SemaphoreType.DMA((8,)),
            pltpu.SemaphoreType.DMA((16,)),
            pltpu.SemaphoreType.DMA((2, N_GX)),
            pltpu.SemaphoreType.DMA((2, N_GX)),
            pltpu.SemaphoreType.DMA((8, 4)),
            pltpu.SemaphoreType.DMA((8, 4)),
        ],
        compiler_params=pltpu.CompilerParams(collective_id=0, has_side_effects=True, vmem_limit_bytes=WHOLE),
        name="exchange",
    )(positions, velocities, masses, smoothing, sound2, counts, move_to, lists)


def share_kernel(own, snd, out, rest_out, own_here, snd_here, rest, load, leave, send, recv):
    u, w = lax.axis_index("gx"), lax.axis_index("gy")
    around = neighbours(u, w)
    barrier = pltpu.get_barrier_semaphore()
    for n in range(8):
        pl.semaphore_signal(barrier, inc=1, device_id=around[n], device_id_type=MESH)
    loads = [pltpu.make_async_copy(own, own_here, load.at[0]), pltpu.make_async_copy(snd.at[0], snd_here, load.at[1])]
    copies = [pltpu.make_async_copy(own, out.at[0], load.at[2])]
    for copy in loads + copies:
        copy.start()
    pl.semaphore_wait(barrier, 8)
    for n in range(8):
        copy = pltpu.make_async_remote_copy(
            src_ref=own, dst_ref=out.at[n + 1], send_sem=send.at[n], recv_sem=recv.at[n],
            device_id=around[n], device_id_type=MESH)
        copy.start()
        copies.append(copy)
    for copy in loads:
        copy.wait()
    fields = extra_fields(snd_here[...], own_here[...])
    for a in range(16):
        columns(rest.at[a], jnp.concatenate([field[a:a + 1] for field in fields], 0), (0, 1, 2))
        copy = pltpu.make_async_copy(rest.at[a], rest_out.at[a], leave.at[a])
        copy.start()
        copies.append(copy)
    for copy in copies:
        copy.wait()


def share(own, snd):
    return pl.pallas_call(
        share_kernel,
        out_shape=(jax.ShapeDtypeStruct((9, 16, 256), jnp.float32), jax.ShapeDtypeStruct((16, 3, 256, 128), jnp.float32)),
        in_specs=[HBM] * 2, out_specs=(HBM,) * 2,
        scratch_shapes=[
            pltpu.VMEM((16, 256), jnp.float32),
            pltpu.VMEM((16, 256), jnp.float32),
            pltpu.VMEM((16, 3, 256, 128), jnp.float32),
            pltpu.SemaphoreType.DMA((3,)),
            pltpu.SemaphoreType.DMA((16,)),
            pltpu.SemaphoreType.DMA((8,)),
            pltpu.SemaphoreType.DMA((8,)),
        ],
        compiler_params=pltpu.CompilerParams(collective_id=1, has_side_effects=True, vmem_limit_bytes=WHOLE),
        name="share",
    )(own, snd)


def body(positions, velocities, masses, smoothing, sound2, counts, move_to, proxy_send, pairs):
    rec, snd, meta, cols = exchange(positions, velocities, masses, smoothing, sound2, counts, move_to, proxy_send.reshape(1, 128))
    rec = rec.reshape(144, 8, 256)
    rho, safe, tab, buf = density(rec, meta, pairs.T, cols)
    rho_all, rest = share(safe, snd)
    accel = force(rec, snd, rho_all, meta, tab, buf, cols, rest)
    return rho, accel


def solution(mesh):
    flat, cells, three = P(("gx", "gy")), P(("gx", "gy"), None), P(None, ("gx", "gy"), None)
    return jax.shard_map(
        body, mesh=mesh,
        in_specs=(three, three, cells, cells, cells, flat, flat, flat, cells),
        out_specs=(cells, three), check_vma=False)
```

time: 116 us -> 112 us (0.966)
  the two profiles are of different devices: /device:TPU:13 before, /device:TPU:0 now
where the time goes in v4:
time: 112 us
  Pallas kernels  112 us (100%)
    pallas_call x1, Pallas kernels, force(): pl.pallas_call(functools.partial(force_kernel, J32, J16, U), out_shape=ja...  48.1 us
    pallas_call x1, Pallas kernels, exchange(): pl.pallas_call(exchange_kernel, out_shape=(jax.ShapeDtypeStruct((9, 16, 8...  27 us
    pallas_call x1, Pallas kernels, density(): pl.pallas_call(functools.partial(density_kernel, J64, J32, J16, U), out_s...  26.6 us
    pallas_call x1, Pallas kernels, share(): pl.pallas_call(share_kernel, out_shape=(jax.ShapeDtypeStruct((9, 16, 256)...  9.83 us

profile of v4, /device:TPU:0, one launch (start us, length us, event | category | flops | bytes accessed | tf_op | source)
XLA Modules:
  0.0 112.2 jit_solution(11134783824945074286)
XLA Ops:
  0.6 27.0 %exchange.1 = (f32[9,16,8,256]{3,2,1,0:T(8,128)}, f32[9,16,256]{2,1,0:T(8,128)}, s32[9,4,128]{2,1,0:T(4,128)}, f32[16,7,256,128]{3,2,1,0:T(8,128)}) custom-call(f32[3,16,256]{2,1,0:T(8,128)} %refs_0_.1, f32[3,16,256]{2,1,0:T(8,128)} %refs_1_.1, f32[16,256]{1,0:T(8,128)} %refs_2_.1, f32[16,256]{1,0:T(8,128)} %refs_3_.1, f32[16,256]{1,0:T(8,128)} %refs_4_.1, ...), custom_call_target="tpu_custom_call" | custom-call | tf_op jit(solution)/shard_map/exchange/pallas_call | solution.py:421
  27.7 26.6 %density.1 = (f32[16,256]{1,0:T(8,128)}, f32[16,256]{1,0:T(8,128)}, s32[384]{0:T(512)}, f32[376,8,128]{2,1,0:T(8,128)}) custom-call(f32[144,8,256]{2,1,0:T(8,128)} %bitcast.3, s32[9,4,128]{2,1,0:T(4,128)} %get-tuple-element.13.meta_in, s32[3,160]{1,0:T(4,128)} %bitcast.5, f32[16,7,256,128]{3,2,1,0:T(8,128)} %get-tuple-element.14.cols_in), custom_call_target="tpu_custom_call" | custom-call | tf_op jit(solution)/shard_map/density/pallas_call | solution.py:132
  54.2 9.8 %share.1 = (f32[9,16,256]{2,1,0:T(8,128)}, f32[16,3,256,128]{3,2,1,0:T(8,128)}) custom-call(f32[16,256]{1,0:T(8,128)} %get-tuple-element.17.own, f32[9,16,256]{2,1,0:T(8,128)} %get-tuple-element.16.snd.snd_in), custom_call_target="tpu_custom_call" | custom-call | tf_op jit(solution)/shard_map/share/pallas_call | solution.py:489
  64.1 48.1 %force.1 = f32[3,16,256]{2,1,0:T(8,128)} custom-call(f32[144,8,256]{2,1,0:T(8,128)} %bitcast.4, f32[9,16,256]{2,1,0:T(8,128)} %get-tuple-element.16.snd.snd_in, f32[9,16,256]{2,1,0:T(8,128)} %get-tuple-element.18.rho_in, s32[9,4,128]{2,1,0:T(4,128)} %get-tuple-element.13.meta_in, s32[384]{0:T(512)} %get-tuple-element.19.tab_in, ...), custom_call_target="tpu_custom_call" | custom-call | tf_op jit(solution)/shard_map/force/pallas_call | solution.py:219

commit v5 on v4

--- a/solution.py
+++ b/solution.py
@@ -214,7 +214,7 @@
             sums=jnp.sum(acc[c,a].T,axis=0,keepdims=True)
             out[c,a:a+1,:]=jnp.where(rec[meta[0,2,a],3:4,:]>0,(160.0*NORM)*sums,0.0)
 
-def force(rec,snd,rho,meta,tab,buf,cols,rest,J32=4,J16=4,U=8):
+def force(rec,snd,rho,meta,tab,buf,cols,rest,J32=4,J16=4,U=16):
     V=pl.BlockSpec(memory_space=pltpu.VMEM); S=pl.BlockSpec(memory_space=pltpu.SMEM); H=pl.BlockSpec(memory_space=pltpu.HBM)
     return pl.pallas_call(functools.partial(force_kernel,J32,J16,U),
         out_shape=jax.ShapeDtypeStruct((3,CELLS,SLOTS),jnp.float32),
@@ -229,6 +229,7 @@
 N_GX=16; N_GY=8
 AROUND=((-1,-1),(-1,0),(-1,1),(0,-1),(0,1),(1,-1),(1,0),(1,1))
 MESH=pl.DeviceIdType.MESH
+FAR_FIRST=(6, 10, 7, 9, 2, 14, 5, 11, 8, 3, 13, 1, 15, 4, 12)
 OWN_FIELDS=(0, 1, 2, 4, 5, 6, 7)
 
 
@@ -296,11 +297,8 @@
             device_id=(lax.rem(u + off, N_GX), w), device_id_type=MESH)
 
     for part in range(2):
-        def start(off, _):
+        for off in FAR_FIRST:
             parcel(off, part).start()
-            return 0
-
-        lax.fori_loop(1, N_GX, start, 0)
     inbox[0] = outbox[0]
     inbox2[0] = outbox2[0]
 
@@ -466,15 +464,15 @@
     copies = [pltpu.make_async_copy(own, out.at[0], load.at[2])]
     for copy in loads + copies:
         copy.start()
+    for copy in loads:
+        copy.wait()
     pl.semaphore_wait(barrier, 8)
     for n in range(8):
         copy = pltpu.make_async_remote_copy(
-            src_ref=own, dst_ref=out.at[n + 1], send_sem=send.at[n], recv_sem=recv.at[n],
+            src_ref=own_here, dst_ref=out.at[n + 1], send_sem=send.at[n], recv_sem=recv.at[n],
             device_id=around[n], device_id_type=MESH)
         copy.start()
         copies.append(copy)
-    for copy in loads:
-        copy.wait()
     fields = extra_fields(snd_here[...], own_here[...])
     for a in range(16):
         columns(rest.at[a], jnp.concatenate([field[a:a + 1] for field in fields], 0), (0, 1, 2))

time: 112 us -> 114 us (1.018)
  the two profiles are of different devices: /device:TPU:0 before, /device:TPU:1 now
where the time goes in v5:
time: 114 us; the launch traced here: 113 us
  Pallas kernels  113 us (99%)
    pallas_call x1, Pallas kernels, force(): pl.pallas_call(functools.partial(force_kernel, J32, J16, U), out_shape=ja...  50.7 us
    pallas_call x1, Pallas kernels, density(): pl.pallas_call(functools.partial(density_kernel, J64, J32, J16, U), out_s...  27.9 us
    pallas_call x1, Pallas kernels, exchange(): pl.pallas_call(exchange_kernel, out_shape=(jax.ShapeDtypeStruct((9, 16, 8...  26.2 us
    pallas_call x1, Pallas kernels, share(): pl.pallas_call(share_kernel, out_shape=(jax.ShapeDtypeStruct((9, 16, 256)...  7.94 us

profile of v5, /device:TPU:1, one launch (start us, length us, event | category | flops | bytes accessed | tf_op | source)
XLA Modules:
  0.0 113.3 jit_solution(11041751322614337646)
XLA Ops:
  0.6 26.2 %exchange.1 = (f32[9,16,8,256]{3,2,1,0:T(8,128)}, f32[9,16,256]{2,1,0:T(8,128)}, s32[9,4,128]{2,1,0:T(4,128)}, f32[16,7,256,128]{3,2,1,0:T(8,128)}) custom-call(f32[3,16,256]{2,1,0:T(8,128)} %refs_0_.1, f32[3,16,256]{2,1,0:T(8,128)} %refs_1_.1, f32[16,256]{1,0:T(8,128)} %refs_2_.1, f32[16,256]{1,0:T(8,128)} %refs_3_.1, f32[16,256]{1,0:T(8,128)} %refs_4_.1, ...), custom_call_target="tpu_custom_call" | custom-call | tf_op jit(solution)/shard_map/exchange/pallas_call | solution.py:419
  26.8 27.9 %density.1 = (f32[16,256]{1,0:T(8,128)}, f32[16,256]{1,0:T(8,128)}, s32[384]{0:T(512)}, f32[376,8,128]{2,1,0:T(8,128)}) custom-call(f32[144,8,256]{2,1,0:T(8,128)} %bitcast.3, s32[9,4,128]{2,1,0:T(4,128)} %get-tuple-element.13.meta_in, s32[3,160]{1,0:T(4,128)} %bitcast.5, f32[16,7,256,128]{3,2,1,0:T(8,128)} %get-tuple-element.14.cols_in), custom_call_target="tpu_custom_call" | custom-call | tf_op jit(solution)/shard_map/density/pallas_call | solution.py:132
  54.7 7.9 %share.1 = (f32[9,16,256]{2,1,0:T(8,128)}, f32[16,3,256,128]{3,2,1,0:T(8,128)}) custom-call(f32[16,256]{1,0:T(8,128)} %get-tuple-element.17.own, f32[9,16,256]{2,1,0:T(8,128)} %get-tuple-element.16.snd.snd_in), custom_call_target="tpu_custom_call" | custom-call | tf_op jit(solution)/shard_map/share/pallas_call | solution.py:487
  62.7 50.7 %force.1 = f32[3,16,256]{2,1,0:T(8,128)} custom-call(f32[144,8,256]{2,1,0:T(8,128)} %bitcast.4, f32[9,16,256]{2,1,0:T(8,128)} %get-tuple-element.16.snd.snd_in, f32[9,16,256]{2,1,0:T(8,128)} %get-tuple-element.18.rho_in, s32[9,4,128]{2,1,0:T(4,128)} %get-tuple-element.13.meta_in, s32[384]{0:T(512)} %get-tuple-element.19.tab_in, ...), custom_call_target="tpu_custom_call" | custom-call | tf_op jit(solution)/shard_map/force/pallas_call | solution.py:219

commit v6 on v5

--- a/solution.py
+++ b/solution.py
@@ -72,7 +72,7 @@
         copy.start()
     return copies
 
-def density_kernel(J64,J32,J16,U,rec_in,meta_in,pairs_in,cols_in,rho,safe,tab,buf_out,rec,meta,pairs,buf,sems,filled,count_of,place_of,shifts,cols,col_sems,acc):
+def density_kernel(J64,JREST,U,rec_in,meta_in,pairs_in,cols_in,rho,safe,tab,buf_out,rec,meta,pairs,buf,sems,filled,count_of,place_of,shifts,cols,col_sems,acc):
     copies=fetch(((meta_in,meta),(pairs_in,pairs),(rec_in,rec)),sems)
     copies[0].wait(); copies[1].wait()
     def column_copy(a):
@@ -92,7 +92,7 @@
         first=tab[FIRST+a]; last=tab[LAST+a]
         count=meta[0,0,a]
         def iblock(IB,JB,start,_):
-            rows=pl.ds(pl.multiple_of(start,16),IB)
+            rows=pl.ds(pl.multiple_of(start,8),IB)
             nfull=(last-first)//JB
             xi,yi,zi,hi=(icol[f,rows,:] for f in range(4))
             def tile(t):
@@ -112,12 +112,12 @@
                 total=lax.fori_loop(first+nfull*JB,last,lambda t,tt:tt+tile(t),total)
             acc[a,rows,:]=total
             return 0
-        groups=lax.shift_right_logical(count+15,4)
-        rest=lax.bitwise_and(groups,3)
-        big=lax.shift_right_logical(groups+1,2)
+        groups=lax.shift_right_logical(count+7,3)
+        rest=lax.bitwise_and(groups,7)
+        big=lax.shift_right_logical(groups,3)-jnp.where(rest==1,1,0)
         lax.fori_loop(0,big,lambda g,c:iblock(64,J64,g*64,c),0)
-        lax.fori_loop(0,jnp.where(rest==2,1,0),lambda g,c:iblock(32,J32,big*64,c),0)
-        lax.fori_loop(0,jnp.where(rest==1,1,0),lambda g,c:iblock(16,J16,big*64,c),0)
+        for r,n in enumerate(JREST,1):
+            lax.fori_loop(0,jnp.where(rest==r,1,0),lambda g,c:iblock(72 if r==1 else 8*r,n,big*64,c),0)
         return 0
     lax.fori_loop(0,CELLS,cell,0)
     for a in range(CELLS):
@@ -127,16 +127,16 @@
         safe[a:a+1,:]=jnp.where(there,(32.0*NORM)*sums,1.0)
     leave.wait()
 
-def density(rec,meta,pairs,cols,J64=2,J32=4,J16=4,U=8):
+def density(rec,meta,pairs,cols,J64=2,JREST=(2,4,4,4,3,2,2),U=8):
     V=pl.BlockSpec(memory_space=pltpu.VMEM); S=pl.BlockSpec(memory_space=pltpu.SMEM); H=pl.BlockSpec(memory_space=pltpu.HBM)
-    return pl.pallas_call(functools.partial(density_kernel,J64,J32,J16,U),
+    return pl.pallas_call(functools.partial(density_kernel,J64,JREST,U),
         out_shape=(jax.ShapeDtypeStruct((CELLS,SLOTS),jnp.float32),jax.ShapeDtypeStruct((CELLS,SLOTS),jnp.float32),jax.ShapeDtypeStruct((384,),jnp.int32),jax.ShapeDtypeStruct((MAXT,8,128),jnp.float32)),
         in_specs=[H,H,H,H],out_specs=(V,V,S,H),
         scratch_shapes=[pltpu.VMEM((144,8,SLOTS),jnp.float32),pltpu.SMEM((9,4,128),jnp.int32),pltpu.SMEM((3,NPAIRS),jnp.int32),pltpu.VMEM((MAXT,8,128),jnp.float32),pltpu.SemaphoreType.DMA((4,)),pltpu.SMEM((CELLS,),jnp.int32),pltpu.SMEM((NPAIRS,),jnp.int32),pltpu.SMEM((NPAIRS,),jnp.int32),pltpu.VMEM((27,8,128),jnp.float32),pltpu.VMEM((CELLS,4,SLOTS,128),jnp.float32),pltpu.SemaphoreType.DMA((CELLS,)),pltpu.VMEM((CELLS,SLOTS,128),jnp.float32)],
         compiler_params=pltpu.CompilerParams(vmem_limit_bytes=WHOLE),
         name="density")(rec,meta,pairs,cols)
 
-def force_kernel(J32,J16,U,rec_in,snd_in,rho_in,meta_in,tab_in,buf_in,cols_in,rest_in,out,rec,snd,rho,meta,tab,buf,sems,extra,cells,cols,col_sems,acc):
+def force_kernel(J32,JREST,U,rec_in,snd_in,rho_in,meta_in,tab_in,buf_in,cols_in,rest_in,out,rec,snd,rho,meta,tab,buf,sems,extra,cells,cols,col_sems,acc):
     copies=fetch(((snd_in,snd),(rho_in,rho),(tab_in,tab),(meta_in.at[0],meta.at[0]),(rec_in.at[pl.ds(0,CELLS)],rec),(buf_in,buf)),sems)
     copies[3].wait()
     def column_copy(a):
@@ -172,7 +172,7 @@
         first=tab[FIRST+a]; last=tab[LAST+a]
         count=meta[0,0,a]
         def iblock(IB,JB,start,_):
-            rows=pl.ds(pl.multiple_of(start,16),IB)
+            rows=pl.ds(pl.multiple_of(start,8),IB)
             nfull=(last-first)//JB
             def tile(t):
                 i=lambda f: cols[a,f,rows,:]
@@ -203,10 +203,12 @@
             for c in range(3):
                 acc[c,a,rows,:]=total[c]
             return 0
-        groups=lax.shift_right_logical(count+15,4)
-        big=lax.shift_right_logical(groups,1)
+        groups=lax.shift_right_logical(count+7,3)
+        rest=lax.bitwise_and(groups,3)
+        big=lax.shift_right_logical(groups,2)-jnp.where(rest==1,1,0)
         lax.fori_loop(0,big,lambda g,c:iblock(32,J32,g*32,c),0)
-        lax.fori_loop(0,lax.bitwise_and(groups,1),lambda g,c:iblock(16,J16,big*32,c),0)
+        for r,n in enumerate(JREST,1):
+            lax.fori_loop(0,jnp.where(rest==r,1,0),lambda g,c:iblock(40 if r==1 else 8*r,n,big*32,c),0)
         return 0
     lax.fori_loop(0,CELLS,cell,0)
     for a in range(CELLS):
@@ -214,9 +216,9 @@
             sums=jnp.sum(acc[c,a].T,axis=0,keepdims=True)
             out[c,a:a+1,:]=jnp.where(rec[meta[0,2,a],3:4,:]>0,(160.0*NORM)*sums,0.0)
 
-def force(rec,snd,rho,meta,tab,buf,cols,rest,J32=4,J16=4,U=16):
+def force(rec,snd,rho,meta,tab,buf,cols,rest,J32=4,JREST=(4,4,4),U=16):
     V=pl.BlockSpec(memory_space=pltpu.VMEM); S=pl.BlockSpec(memory_space=pltpu.SMEM); H=pl.BlockSpec(memory_space=pltpu.HBM)
-    return pl.pallas_call(functools.partial(force_kernel,J32,J16,U),
+    return pl.pallas_call(functools.partial(force_kernel,J32,JREST,U),
         out_shape=jax.ShapeDtypeStruct((3,CELLS,SLOTS),jnp.float32),
         in_specs=[H]*8,out_specs=V,
         scratch_shapes=[pltpu.VMEM((CELLS,8,SLOTS),jnp.float32),pltpu.VMEM((9,CELLS,SLOTS),jnp.float32),pltpu.VMEM((9,CELLS,SLOTS),jnp.float32),pltpu.SMEM((1,4,128),jnp.int32),pltpu.SMEM((384,),jnp.int32),pltpu.VMEM((MAXT,8,128),jnp.float32),pltpu.SemaphoreType.DMA((6,)),pltpu.VMEM((MAXT,8,128),jnp.float32),pltpu.VMEM((2,144*8,128),jnp.float32),pltpu.VMEM((CELLS,10,SLOTS,128),jnp.float32),pltpu.SemaphoreType.DMA((2,CELLS)),pltpu.VMEM((3,CELLS,SLOTS,128),jnp.float32)],

time: 114 us -> 114 us (level)
  the two profiles are of different devices: /device:TPU:1 before, /device:TPU:4 now
where the time goes in v6:
time: 114 us; the launch traced here: 113 us
  Pallas kernels  113 us (99%)
    pallas_call x1, Pallas kernels, force(): pl.pallas_call(functools.partial(force_kernel, J32, JREST, U), out_shape=...  51.8 us
    pallas_call x1, Pallas kernels, density(): pl.pallas_call(functools.partial(density_kernel, J64, JREST, U), out_shap...  28.5 us
    pallas_call x1, Pallas kernels, exchange(): pl.pallas_call(exchange_kernel, out_shape=(jax.ShapeDtypeStruct((9, 16, 8...  24.1 us
    pallas_call x1, Pallas kernels, share(): pl.pallas_call(share_kernel, out_shape=(jax.ShapeDtypeStruct((9, 16, 256)...  8.27 us

profile of v6, /device:TPU:4, one launch (start us, length us, event | category | flops | bytes accessed | tf_op | source)
XLA Modules:
  0.0 113.4 jit_solution(11690464143878401314)
XLA Ops:
  0.6 24.1 %exchange.1 = (f32[9,16,8,256]{3,2,1,0:T(8,128)}, f32[9,16,256]{2,1,0:T(8,128)}, s32[9,4,128]{2,1,0:T(4,128)}, f32[16,7,256,128]{3,2,1,0:T(8,128)}) custom-call(f32[3,16,256]{2,1,0:T(8,128)} %refs_0_.1, f32[3,16,256]{2,1,0:T(8,128)} %refs_1_.1, f32[16,256]{1,0:T(8,128)} %refs_2_.1, f32[16,256]{1,0:T(8,128)} %refs_3_.1, f32[16,256]{1,0:T(8,128)} %refs_4_.1, ...), custom_call_target="tpu_custom_call" | custom-call | tf_op jit(solution)/shard_map/exchange/pallas_call | solution.py:421
  24.8 28.5 %density.1 = (f32[16,256]{1,0:T(8,128)}, f32[16,256]{1,0:T(8,128)}, s32[384]{0:T(512)}, f32[376,8,128]{2,1,0:T(8,128)}) custom-call(f32[144,8,256]{2,1,0:T(8,128)} %bitcast.3, s32[9,4,128]{2,1,0:T(4,128)} %get-tuple-element.13.meta_in, s32[3,160]{1,0:T(4,128)} %bitcast.5, f32[16,7,256,128]{3,2,1,0:T(8,128)} %get-tuple-element.14.cols_in), custom_call_target="tpu_custom_call" | custom-call | tf_op jit(solution)/shard_map/density/pallas_call | solution.py:132
  53.3 8.3 %share.1 = (f32[9,16,256]{2,1,0:T(8,128)}, f32[16,3,256,128]{3,2,1,0:T(8,128)}) custom-call(f32[16,256]{1,0:T(8,128)} %get-tuple-element.17.own, f32[9,16,256]{2,1,0:T(8,128)} %get-tuple-element.16.snd.snd_in), custom_call_target="tpu_custom_call" | custom-call | tf_op jit(solution)/shard_map/share/pallas_call | solution.py:489
  61.6 51.8 %force.1 = f32[3,16,256]{2,1,0:T(8,128)} custom-call(f32[144,8,256]{2,1,0:T(8,128)} %bitcast.4, f32[9,16,256]{2,1,0:T(8,128)} %get-tuple-element.16.snd.snd_in, f32[9,16,256]{2,1,0:T(8,128)} %get-tuple-element.18.rho_in, s32[9,4,128]{2,1,0:T(4,128)} %get-tuple-element.13.meta_in, s32[384]{0:T(512)} %get-tuple-element.19.tab_in, ...), custom_call_target="tpu_custom_call" | custom-call | tf_op jit(solution)/shard_map/force/pallas_call | solution.py:221

commit v7 on v6

--- a/solution.py
+++ b/solution.py
@@ -127,7 +127,7 @@
         safe[a:a+1,:]=jnp.where(there,(32.0*NORM)*sums,1.0)
     leave.wait()
 
-def density(rec,meta,pairs,cols,J64=2,JREST=(2,4,4,4,3,2,2),U=8):
+def density(rec,meta,pairs,cols,J64=2,JREST=(2,4,4,4,3,2,2),U=16):
     V=pl.BlockSpec(memory_space=pltpu.VMEM); S=pl.BlockSpec(memory_space=pltpu.SMEM); H=pl.BlockSpec(memory_space=pltpu.HBM)
     return pl.pallas_call(functools.partial(density_kernel,J64,JREST,U),
         out_shape=(jax.ShapeDtypeStruct((CELLS,SLOTS),jnp.float32),jax.ShapeDtypeStruct((CELLS,SLOTS),jnp.float32),jax.ShapeDtypeStruct((384,),jnp.int32),jax.ShapeDtypeStruct((MAXT,8,128),jnp.float32)),

time: 114 us -> 109 us (0.956)
  the two profiles are of different devices: /device:TPU:4 before, /device:TPU:26 now
where the time goes in v7:
time: 109 us
  Pallas kernels  109 us (100%)
    pallas_call x1, Pallas kernels, force(): pl.pallas_call(functools.partial(force_kernel, J32, JREST, U), out_shape=...  49.5 us
    pallas_call x1, Pallas kernels, density(): pl.pallas_call(functools.partial(density_kernel, J64, JREST, U), out_shap...  27.1 us
    pallas_call x1, Pallas kernels, exchange(): pl.pallas_call(exchange_kernel, out_shape=(jax.ShapeDtypeStruct((9, 16, 8...  25 us
    pallas_call x1, Pallas kernels, share(): pl.pallas_call(share_kernel, out_shape=(jax.ShapeDtypeStruct((9, 16, 256)...  7.06 us

profile of v7, /device:TPU:26, one launch (start us, length us, event | category | flops | bytes accessed | tf_op | source)
XLA Modules:
  0.0 109.3 jit_solution(75809288752622665)
XLA Ops:
  0.6 25.0 %exchange.1 = (f32[9,16,8,256]{3,2,1,0:T(8,128)}, f32[9,16,256]{2,1,0:T(8,128)}, s32[9,4,128]{2,1,0:T(4,128)}, f32[16,7,256,128]{3,2,1,0:T(8,128)}) custom-call(f32[3,16,256]{2,1,0:T(8,128)} %refs_0_.1, f32[3,16,256]{2,1,0:T(8,128)} %refs_1_.1, f32[16,256]{1,0:T(8,128)} %refs_2_.1, f32[16,256]{1,0:T(8,128)} %refs_3_.1, f32[16,256]{1,0:T(8,128)} %refs_4_.1, ...), custom_call_target="tpu_custom_call" | custom-call | tf_op jit(solution)/shard_map/exchange/pallas_call | solution.py:421
  25.6 27.1 %density.1 = (f32[16,256]{1,0:T(8,128)}, f32[16,256]{1,0:T(8,128)}, s32[384]{0:T(512)}, f32[376,8,128]{2,1,0:T(8,128)}) custom-call(f32[144,8,256]{2,1,0:T(8,128)} %bitcast.3, s32[9,4,128]{2,1,0:T(4,128)} %get-tuple-element.13.meta_in, s32[3,160]{1,0:T(4,128)} %bitcast.5, f32[16,7,256,128]{3,2,1,0:T(8,128)} %get-tuple-element.14.cols_in), custom_call_target="tpu_custom_call" | custom-call | tf_op jit(solution)/shard_map/density/pallas_call | solution.py:132
  52.7 7.1 %share.1 = (f32[9,16,256]{2,1,0:T(8,128)}, f32[16,3,256,128]{3,2,1,0:T(8,128)}) custom-call(f32[16,256]{1,0:T(8,128)} %get-tuple-element.17.own, f32[9,16,256]{2,1,0:T(8,128)} %get-tuple-element.16.snd.snd_in), custom_call_target="tpu_custom_call" | custom-call | tf_op jit(solution)/shard_map/share/pallas_call | solution.py:489
  59.8 49.5 %force.1 = f32[3,16,256]{2,1,0:T(8,128)} custom-call(f32[144,8,256]{2,1,0:T(8,128)} %bitcast.4, f32[9,16,256]{2,1,0:T(8,128)} %get-tuple-element.16.snd.snd_in, f32[9,16,256]{2,1,0:T(8,128)} %get-tuple-element.18.rho_in, s32[9,4,128]{2,1,0:T(4,128)} %get-tuple-element.13.meta_in, s32[384]{0:T(512)} %get-tuple-element.19.tab_in, ...), custom_call_target="tpu_custom_call" | custom-call | tf_op jit(solution)/shard_map/force/pallas_call | solution.py:221
